TPU v7x, 512 devices: a whole 4x8x8 slice. The times are simulated.
512 devices in a mesh: rows: 128 (over z, y, core), grp: 4 (over x).
Axes of the slice: x: 4, y: 8, z: 8, core: 2. Of those that a mesh axis runs over, the one named last changes fastest.
Arguments:
- slab: float32 [4, 65536, 256], P('grp', 'rows'), as said below
- buckets: int32 [4, 65536], P('grp', 'rows'), may hold values from 0 to 255
- signs: int32 [4, 65536], P('grp', 'rows'), may hold values from -1 to 1, as said below
- counts: int32 [4, 16384], P('grp', 'rows'), may hold values from 1 to 4
Outputs:
- sketch: float32 [4, 32768, 256], P('grp', 'rows')
- factor: float32 [256, 256], replicated
Inputs may be any that keep to these rules, and one draw needn't show every extreme that they name: Rows of the slab have varied scales and correlated columns. `signs`: each entry is -1 or +1.
All inputs are finite; a program needn't handle non-finite values.
Results may differ from a plain program's by a relative error of at most 0.0003.
Values sent between devices are 32-bit elements; how exact they have to be, the bound alone decides.
A program may use at most 64 MiB of HBM per device.

v0:
```python
import jax
import jax.numpy as jnp
from jax import lax
from jax.sharding import PartitionSpec as P

BPO = 256


def body(slab, buckets, signs, counts):
    owners = lax.axis_size("rows")
    width = slab.shape[2]
    capacity = slab.shape[1] // owners
    blocks = slab.reshape(owners, capacity, width)
    bucket_ids = buckets.reshape(owners, capacity)
    sign_ids = signs.reshape(owners, capacity)
    used_counts = counts.reshape(owners, 1)
    place = lax.broadcasted_iota(jnp.int32, (owners, capacity), 1)
    got_rows, got_buckets, got_signs, got_counts = (
        lax.all_to_all(blocks, "rows", split_axis=0, concat_axis=0, tiled=True),
        lax.all_to_all(bucket_ids, "rows", split_axis=0, concat_axis=0, tiled=True),
        lax.all_to_all(sign_ids, "rows", split_axis=0, concat_axis=0, tiled=True),
        lax.all_to_all(used_counts, "rows", split_axis=0, concat_axis=0, tiled=True),
    )
    weight = jnp.where(place < got_counts, got_signs, 0).astype(jnp.float32)
    weighted = got_rows * weight[:, :, None]
    flat_rows = weighted.reshape(owners * capacity, width)
    flat_ids = got_buckets.reshape(1, owners * capacity)
    onehot = (lax.broadcasted_iota(jnp.int32, (BPO, owners * capacity), 0) == flat_ids).astype(
        jnp.float32
    )
    local_sketch = jnp.dot(
        onehot, flat_rows, precision=lax.Precision.HIGHEST, preferred_element_type=jnp.float32
    )
    total_slots = float(lax.axis_size("grp") * owners * owners * capacity)
    local_gram = jnp.dot(
        local_sketch.T,
        local_sketch,
        precision=lax.Precision.HIGHEST,
        preferred_element_type=jnp.float32,
    )
    gram = lax.psum(local_gram, ("rows", "grp"))
    factor = jnp.linalg.cholesky(gram / total_slots).T
    return (local_sketch.reshape(1, BPO, width), factor)


def solution(mesh):
    in_specs = (P("grp", "rows", None), P("grp", "rows"), P("grp", "rows"), P("grp", "rows"))
    out_specs = (P("grp", "rows", None), P())
    return jax.shard_map(body, mesh=mesh, in_specs=in_specs, out_specs=out_specs, check_vma=False)
```

profile of v0, /device:TPU:1, one launch (start us, length us, event | category | flops | bytes accessed | tf_op | source)
XLA Modules:
  0.0 407.3 jit_solution(9158817283218652099)
XLA Ops:
  7.2 0.0 copy-start.3
  7.2 0.0 copy-start.2
  7.2 0.6 copy-done.3
  7.8 0.7 copy.19
  8.6 18.4 %all-to-all-start.2 = ((s32[128,1,1]{2,1,0:T(1,128)}), s32[128,1,1]{2,1,0:T(1,128)S(1)}, u32[]{:S(2)}, u32[]{:S(2)}) async-start(s32[128,1,1]{2,1,0:T(1,128)} %copy.19), calls=%async_computation.2 | async-start | bytes 131072 | tf_op jit(solution)/shard_map/all_to_all | solution.py:22
  27.0 0.6 broadcast.105
  27.6 1.4 reduce.22
  29.0 0.7 all_to_all.28
  29.7 8.7 %all-to-all-done.2 = s32[128,1,1]{2,1,0:T(1,128)S(1)} async-done(((s32[128,1,1]{2,1,0:T(1,128)}), s32[128,1,1]{2,1,0:T(1,128)S(1)}, u32[]{:S(2)}, u32[]{:S(2)}) %all-to-all-start.2) | async-done | bytes 544 | tf_op jit(solution)/shard_map/all_to_all | solution.py:22
  38.4 5.7 %all-to-all-start.3 = ((s32[128,1,4]{2,1,0:T(1,128)}), s32[128,1,4]{2,1,0:T(1,128)S(1)}, u32[]{:S(2)}, u32[]{:S(2)}) async-start(s32[128,1,4]{2,1,0:T(1,128)} %bitcast.2), calls=%async_computation.3 | async-start | bytes 131072 | tf_op jit(solution)/shard_map/all_to_all | solution.py:21
  44.1 1.4 reduce.23
  45.5 0.7 all_to_all.23
  46.2 9.4 %all-to-all-done.3 = s32[128,1,4]{2,1,0:T(1,128)S(1)} async-done(((s32[128,1,4]{2,1,0:T(1,128)}), s32[128,1,4]{2,1,0:T(1,128)S(1)}, u32[]{:S(2)}, u32[]{:S(2)}) %all-to-all-start.3) | async-done | bytes 2080 | tf_op jit(solution)/shard_map/all_to_all | solution.py:21
  55.6 5.7 %all-to-all-start = ((s32[128,1,4]{2,1,0:T(1,128)}), s32[128,1,4]{2,1,0:T(1,128)S(1)}, u32[]{:S(2)}, u32[]{:S(2)}) async-start(s32[128,1,4]{2,1,0:T(1,128)} %bitcast), calls=%async_computation | async-start | bytes 131072 | tf_op jit(solution)/shard_map/all_to_all | solution.py:20
  61.3 0.0 copy-done.2
  61.3 0.9 reshape.69
  62.3 10.5 %all-to-all-done = s32[128,1,4]{2,1,0:T(1,128)S(1)} async-done(((s32[128,1,4]{2,1,0:T(1,128)}), s32[128,1,4]{2,1,0:T(1,128)S(1)}, u32[]{:S(2)}, u32[]{:S(2)}) %all-to-all-start) | async-done | bytes 2080 | tf_op jit(solution)/shard_map/all_to_all | solution.py:20
  72.8 5.7 %all-to-all-start.1 = ((f32[128,4,256]{2,1,0:T(4,128)}), f32[128,4,256]{2,1,0:T(4,128)S(1)}, u32[]{:S(2)}, u32[]{:S(2)}) async-start(f32[128,4,256]{2,1,0:T(4,128)} %reshape.69), calls=%async_computation.1 | async-start | bytes 1048576 | tf_op jit(solution)/shard_map/all_to_all | solution.py:19
  78.6 0.2 all-reduce.3.cloned.1.call-start
  78.8 2.4 reduce.14
  81.2 0.9 reduce.24
  82.0 0.1 eq.10
  82.1 0.1 select_convert_fusion
  82.2 17.0 %all-to-all-done.1 = f32[128,4,256]{2,1,0:T(4,128)S(1)} async-done(((f32[128,4,256]{2,1,0:T(4,128)}), f32[128,4,256]{2,1,0:T(4,128)S(1)}, u32[]{:S(2)}, u32[]{:S(2)}) %all-to-all-start.1) | async-done | bytes 524320 | tf_op jit(solution)/shard_map/all_to_all | solution.py:19
  99.3 0.2 broadcast_multiply_fusion
  99.5 0.2 reshape.70
  99.7 0.5 fusion
  100.1 0.0 copy-start
  100.1 1.3 fusion.6
  101.4 0.0 copy-done
  101.4 0.0 all-reduce.3.cloned.1.call-update
  101.5 260.2 %all-reduce.3.cloned.1.call-done = f32[256,256]{0,1:T(8,128)} async-done(((f32[256,256]{0,1:T(8,128)}), f32[256,256]{0,1:T(8,128)}) %all-reduce.3.cloned.1.call-update) | async-done | bytes 262160 | tf_op jit(solution)/shard_map/psum | solution.py:41
  361.7 1.0 broadcast_multiply_fusion.1
  362.7 0.0 copy-start.1
  362.7 0.1 copy.22
  362.8 0.8 copy-done.1
  363.7 11.7 %cholesky.50 = f32[128,128]{1,0:T(8,128)S(1)} custom-call(f32[128,128]{1,0:T(8,128)S(1)} %cholesky.118), custom_call_target="Cholesky" | custom-call | tf_op jit(solution)/shard_map/jit(cholesky)/cholesky | solution.py:42
  375.4 9.8 %custom-call.11 = f32[1,128,128]{1,2,0:T(8,128)S(1)} custom-call(f32[1,128,128]{2,1,0:T(8,128)S(1)} %get-tuple-element.13), custom_call_target="InvertDiagBlocksLowerTriangular" | custom-call | tf_op jit(solution)/shard_map/jit(cholesky)/cholesky | solution.py:42
  385.3 0.2 constant_dynamic-update-slice_fusion.1
  385.5 0.3 convolution_subtract_fusion
  385.7 11.7 %cholesky.105 = f32[128,128]{1,0:T(8,128)S(1)} custom-call(f32[128,128]{1,0:T(8,128)S(1)} %convolution_subtract_fusion), custom_call_target="Cholesky" | custom-call | tf_op jit(solution)/shard_map/jit(cholesky)/cholesky | solution.py:42
  397.5 0.7 compare_reduce_fusion
  399.6 0.8 copy.23
  (6 shorter events, 0.2 us)
Async XLA Ops:
  7.2 0.7 copy-start.3
  7.2 54.2 %copy-start.2 = (f32[1,512,256]{2,1,0:T(8,128)S(1)}, f32[1,512,256]{2,1,0:T(8,128)}, u32[]{:S(2)}) copy-start(f32[1,512,256]{2,1,0:T(8,128)} %param.4) | copy-start | bytes 1572868
  8.6 29.8 %all-to-all-start.2 = ((s32[128,1,1]{2,1,0:T(1,128)}), s32[128,1,1]{2,1,0:T(1,128)S(1)}, u32[]{:S(2)}, u32[]{:S(2)}) async-start(s32[128,1,1]{2,1,0:T(1,128)} %copy.19), calls=%async_computation.2 | async-start | bytes 131072 | tf_op jit(solution)/shard_map/all_to_all | solution.py:22
  38.4 17.2 %all-to-all-start.3 = ((s32[128,1,4]{2,1,0:T(1,128)}), s32[128,1,4]{2,1,0:T(1,128)S(1)}, u32[]{:S(2)}, u32[]{:S(2)}) async-start(s32[128,1,4]{2,1,0:T(1,128)} %bitcast.2), calls=%async_computation.3 | async-start | bytes 131072 | tf_op jit(solution)/shard_map/all_to_all | solution.py:21
  55.6 17.2 %all-to-all-start = ((s32[128,1,4]{2,1,0:T(1,128)}), s32[128,1,4]{2,1,0:T(1,128)S(1)}, u32[]{:S(2)}, u32[]{:S(2)}) async-start(s32[128,1,4]{2,1,0:T(1,128)} %bitcast), calls=%async_computation | async-start | bytes 131072 | tf_op jit(solution)/shard_map/all_to_all | solution.py:20
  72.8 26.4 %all-to-all-start.1 = ((f32[128,4,256]{2,1,0:T(4,128)}), f32[128,4,256]{2,1,0:T(4,128)S(1)}, u32[]{:S(2)}, u32[]{:S(2)}) async-start(f32[128,4,256]{2,1,0:T(4,128)} %reshape.69), calls=%async_computation.1 | async-start | bytes 1048576 | tf_op jit(solution)/shard_map/all_to_all | solution.py:19
  78.6 283.1 %all-reduce.3.cloned.1.call-start = ((), (), s32[]{:S(2)}) async-start(), calls=%async_computation.4 | async-start | bytes 524288 | tf_op jit(solution)/shard_map/psum | solution.py:41
  100.1 1.3 copy-start
  362.7 1.0 copy-start.1
Sparse Core Ops, SparseCore 0:
  101.6 260.0 all-reduce.2
where the time goes:
time: 408 us; the launch traced here: 407 us
  waiting for transfers between devices  306 us (75%)
  other arithmetic  41.3 us (10%)
  starting transfers between devices  35.8 us (9%)
  between operations  15.5 us (4%)
  local copies, waits for them, and re-layouts  6.48 us (2%)
    psum x1, waiting for transfers between devices, body(): gram = lax.psum(local_gram, ('rows', 'grp'))  260 us
    another operation x6, other arithmetic, body(): factor = jnp.linalg.cholesky(gram / total_slots).T  34 us
    all_to_all x1, starting transfers between devices, body(): lax.all_to_all(used_counts, 'rows', split_axis=0, concat_axis=0, tiled=True)  18.4 us
    all_to_all x1, waiting for transfers between devices, body(): lax.all_to_all(blocks, 'rows', split_axis=0, concat_axis=0, tiled=True)  17 us
    all_to_all x1, waiting for transfers between devices, body(): lax.all_to_all(bucket_ids, 'rows', split_axis=0, concat_axis=0, tiled=True)  10.5 us
    all_to_all x1, waiting for transfers between devices, body(): lax.all_to_all(sign_ids, 'rows', split_axis=0, concat_axis=0, tiled=True)  9.36 us
    all_to_all x1, waiting for transfers between devices, body(): lax.all_to_all(used_counts, 'rows', split_axis=0, concat_axis=0, tiled=True)  8.66 us
  transfers between devices with their start and end apart: 5, of which 5 were waited for; matrix products, arithmetic and copies ran while one was open for 2% of the time, Pallas kernels for 0%

commit v1 on v0

v1 whole, which is shorter than its diff:
```python
import jax
import jax.numpy as jnp
from jax import lax
from jax.experimental import pallas as pl
from jax.experimental.pallas import tpu as pltpu
from jax.sharding import PartitionSpec as P

NZ = 8
NY = 8
NX = 4
BPO = 256
HALF = 128
F32 = jnp.float32
BF16 = jnp.bfloat16
MESH = pl.DeviceIdType.MESH
ORDER = (4, 3, 5, 2, 6, 1, 7)


def gram_kernel(
    slab, meta, sk_out, g_out,
    r1a, r1b, r2a, r2b, m1, m2, mt, gp, gc, gh, gz, acc, gy, part, gx, fin, gfull,
    loc_sem, s1a_s, s1a_r, s1b_s, s1b_r, s1m_s, s1m_r, s2a_s, s2a_r, s2b_s, s2b_r, s2m_s, s2m_r,
    c_s, c_r, z_s, z_r, y_s, y_r, x_s, x_r, yg_s, yg_r, zg_s, zg_r, cg_s, cg_r,
):
    r = lax.axis_index("rows")
    x = lax.axis_index("grp")
    z = r // 16
    y = (r // 2) % 8
    c = r % 2
    oc = 1 - c

    def dev(zz, yy, cc, xx):
        return ((zz * NY + yy) * 2 + cc, xx)

    barrier = pltpu.get_barrier_semaphore()
    peers = [dev(z, y, oc, x)]
    for d in range(1, 8):
        for dc in range(2):
            peers.append(dev((z + d) % NZ, y, (c + dc) % 2, x))
            peers.append(dev(z, (y + d) % NY, (c + dc) % 2, x))
    for d in range(1, 4):
        peers.append(dev(z, y, c, (x + d) % NX))
    for p in peers:
        pl.semaphore_signal(barrier, inc=1, device_id=p, device_id_type=MESH)

    sends = []

    def rcopy(src, dst, ss, rs, to):
        cp = pltpu.make_async_remote_copy(
            src_ref=src, dst_ref=dst, send_sem=ss, recv_sem=rs, device_id=to, device_id_type=MESH
        )
        cp.start()
        sends.append(cp)
        return cp

    def lcopy(src, dst, sem):
        cp = pltpu.make_async_copy(src, dst, sem)
        cp.start()
        return cp

    la = lcopy(slab.at[z, :, :, pl.ds(0, HALF)], r1a.at[z], loc_sem.at[0])
    lb = lcopy(slab.at[:, y, :, pl.ds(HALF, HALF)], r1b.at[y], loc_sem.at[1])
    lm = lcopy(meta.at[pl.ds(z, 1)], m1.at[pl.ds(z, 1)], loc_sem.at[2])
    pl.semaphore_wait(barrier, len(peers))

    in_m, in_a, in_b = [], [], []
    for d in ORDER:
        zt = (z + d) % NZ
        in_m.append(rcopy(meta.at[pl.ds(zt, 1)], m1.at[pl.ds(z, 1)], s1m_s.at[d], s1m_r.at[d], dev(zt, y, c, x)))
    for d in ORDER:
        zt = (z + d) % NZ
        yt = (y + d) % NY
        in_a.append(rcopy(slab.at[zt, :, :, pl.ds(0, HALF)], r1a.at[z], s1a_s.at[d], s1a_r.at[d], dev(zt, y, c, x)))
        in_b.append(rcopy(slab.at[:, yt, :, pl.ds(HALF, HALF)], r1b.at[y], s1b_s.at[d], s1b_r.at[d], dev(z, yt, c, x)))

    lm.wait()
    for cp in in_m:
        cp.wait_recv()
    arrive = []
    for d in ORDER + (0,):
        for dc in range(2):
            if d == 0 and dc == 0:
                continue
            to = dev(z, (y + d) % NY, (c + dc) % 2, x)
            arrive.append(rcopy(m1, m2.at[c, y], s2m_s.at[d * 2 + dc], s2m_r.at[d * 2 + dc], to))
    m2[c, y] = m1[...]

    la.wait()
    for cp in in_a:
        cp.wait_recv()
    for d in ORDER + (0,):
        for dc in range(2):
            if d == 0 and dc == 0:
                continue
            yt = (y + d) % NY
            ct = (c + dc) % 2
            arrive.append(rcopy(
                r1a.at[:, yt, pl.ds(ct * 4, 4), :], r2a.at[y, :, pl.ds(c * 4, 4), :],
                s2a_s.at[d * 2 + dc], s2a_r.at[d * 2 + dc], dev(z, yt, ct, x),
            ))
    l2a = lcopy(r1a.at[:, y, pl.ds(c * 4, 4), :], r2a.at[y, :, pl.ds(c * 4, 4), :], loc_sem.at[3])
    lb.wait()
    for cp in in_b:
        cp.wait_recv()
    for d in ORDER + (0,):
        for dc in range(2):
            if d == 0 and dc == 0:
                continue
            zt = (z + d) % NZ
            ct = (c + dc) % 2
            arrive.append(rcopy(
                r1b.at[:, zt, pl.ds(ct * 4, 4), :], r2b.at[:, z, pl.ds(c * 4, 4), :],
                s2b_s.at[d * 2 + dc], s2b_r.at[d * 2 + dc], dev(zt, y, ct, x),
            ))
    l2b = lcopy(r1b.at[:, z, pl.ds(c * 4, 4), :], r2b.at[:, z, pl.ds(c * 4, 4), :], loc_sem.at[4])

    n_m = 15
    for cp in arrive[:n_m]:
        cp.wait_recv()
    mt[...] = jnp.transpose(m2[...].reshape(128, 128))
    b4 = mt[pl.ds(y * 8 + c * 4, 4), :]
    w4 = mt[pl.ds(64 + y * 8 + c * 4, 4), :]
    row = lax.broadcasted_iota(jnp.int32, (BPO, 128), 0)
    onehot = jnp.concatenate(
        [jnp.where(row == b4[s:s + 1, :], w4[s:s + 1, :], 0).astype(F32) for s in range(4)], axis=1
    ).astype(BF16)

    for cp in arrive[n_m:]:
        cp.wait_recv()
    l2a.wait()
    l2b.wait()
    fa = r2a.reshape(512, 128)
    fb = r2b.reshape(512, 128)
    rows = jnp.concatenate(
        [
            jnp.concatenate([f[pl.ds(k * 4 + s, 64, stride=8), :] for s in range(4) for k in range(2)], axis=0)
            for f in (fa, fb)
        ],
        axis=1,
    )
    hi = rows.astype(BF16)
    rest = rows - hi.astype(F32)
    mid = rest.astype(BF16)
    low = (rest - mid.astype(F32)).astype(BF16)
    sketch = jnp.dot(onehot, low, preferred_element_type=F32)
    sketch = sketch + jnp.dot(onehot, mid, preferred_element_type=F32)
    sketch = sketch + jnp.dot(onehot, hi, preferred_element_type=F32)
    sk_out[...] = sketch

    def outer(a, b):
        return lax.dot_general(
            a, b, (((0,), (0,)), ((), ())), precision=lax.Precision.HIGHEST, preferred_element_type=F32
        )

    left = sketch[:, :HALF]
    right = sketch[:, HALF:]
    gp[pl.ds(0, 128), :] = outer(left, left)
    gp[pl.ds(128, 128), :] = outer(left, right)
    gp[pl.ds(256, 128), :] = outer(right, right)

    sib = dev(z, y, oc, x)
    rcopy(gp.at[pl.ds(oc * 192, 192)], gc, c_s, c_r, sib).wait_recv()
    gh[...] = gp[pl.ds(pl.multiple_of(c * 192, 8), 192), :] + gc[...]

    got = []
    for d in ORDER:
        zt = (z + d) % NZ
        got.append(rcopy(gh.at[pl.ds(zt * 24, 24)], gz.at[d], z_s.at[d], z_r.at[d], dev(zt, y, c, x)))
    total = gh[pl.ds(pl.multiple_of(z * 24, 8), 24), :]
    for d, cp in zip(ORDER, got):
        cp.wait_recv()
        total = total + gz[d]
    acc[...] = total

    got = []
    for d in ORDER:
        yt = (y + d) % NY
        got.append(rcopy(acc.at[pl.ds(yt * 3, 3)], gy.at[d, pl.ds(0, 3)], y_s.at[d], y_r.at[d], dev(z, yt, c, x)))
    total = acc[pl.ds(y * 3, 3), :]
    for d, cp in zip(ORDER, got):
        cp.wait_recv()
        total = total + gy[d, 0:3]
    part[0:3, :] = total

    got = []
    for d in (2, 1, 3):
        xt = (x + d) % NX
        got.append(rcopy(part.at[pl.ds(0, 3)], gx.at[x, pl.ds(0, 3)], x_s.at[d], x_r.at[d], dev(z, y, c, xt)))
    gx[x, 0:3] = total
    for cp in got:
        cp.wait_recv()
    total = (gx[0, 0:3] + gx[1, 0:3]) + (gx[2, 0:3] + gx[3, 0:3])
    fin[pl.ds(y * 3, 3), :] = total

    got = []
    for d in ORDER:
        yt = (y + d) % NY
        got.append(rcopy(fin.at[pl.ds(y * 3, 3)], fin.at[pl.ds(y * 3, 3)], yg_s.at[d], yg_r.at[d], dev(z, yt, c, x)))
    for cp in got:
        cp.wait_recv()

    def place(zz):
        return gfull.at[pl.ds(c * 192 + zz * 24, 24)]

    got = []
    for d in ORDER:
        zt = (z + d) % NZ
        got.append(rcopy(fin, place(z), zg_s.at[d], zg_r.at[d], dev(zt, y, c, x)))
    over = [rcopy(fin, place(z), cg_s.at[0], cg_r.at[0], sib)]
    gfull[pl.ds(pl.multiple_of(c * 192 + z * 24, 8), 24), :] = fin[...]
    for d, cp in reversed(list(zip(ORDER, got))):
        cp.wait_recv()
        piece = place((z - d) % NZ)
        over.append(rcopy(piece, piece, cg_s.at[d], cg_r.at[d], sib))
    for cp in over:
        cp.wait_recv()
    g_out[...] = gfull[...]
    for cp in sends:
        cp.wait_send()


def factor_block(groups, lanes, n_lane_tiles, k0, emit):
    groups = list(groups)
    n = len(groups)
    for p in range(n):
        base = p * 8
        cols = [
            [jnp.broadcast_to(g[:, base + j:base + j + 1], (8, 128)) for j in range(8)] for g in groups[p:]
        ]
        diag = [[jnp.broadcast_to(cols[0][j][i:i + 1, :], (8, 128)) for j in range(i + 1)] for i in range(8)]
        low = [[None] * 8 for _ in range(8)]
        inv = []
        for j in range(8):
            rj = lax.rsqrt(diag[j][j])
            inv.append(rj)
            for i in range(j + 1, 8):
                low[i][j] = diag[i][j] * rj
            for i in range(j + 1, 8):
                for jj in range(j + 1, i + 1):
                    diag[i][jj] = diag[i][jj] - low[i][j] * low[jj][j]
        lead = groups[p]
        width = lead.shape[1]
        out = []
        inv_w = [jnp.concatenate([v] * (width // 128), axis=1) for v in inv]
        low_w = [[None if v is None else jnp.concatenate([v] * (width // 128), axis=1) for v in lr] for lr in low]
        for j in range(8):
            row = jnp.broadcast_to(lead[j:j + 1, :], (8, width))
            for i in range(j):
                row = row - low_w[j][i] * out[i]
            out.append(row * inv_w[j])
        for j in range(8):
            emit(k0 + base + j, base + j, out[j][0:1, :])
        for g in range(p + 1, n):
            mult = []
            for j in range(8):
                v = cols[g - p][j]
                for i in range(j):
                    v = v - low[j][i] * mult[i]
                mult.append(v * inv[j])
            upd = groups[g]
            for j in range(8):
                mw = jnp.concatenate([mult[j]] * (width // 128), axis=1)
                upd = upd - mw * out[j]
            groups[g] = upd


def factor_kernel(scale, g_ref, sk_ref, f_out, sk_out, sem):
    cp = pltpu.make_async_copy(sk_ref, sk_out, sem)
    cp.start()
    lane2 = lax.broadcasted_iota(jnp.int32, (1, 256), 1)
    lane1 = lax.broadcasted_iota(jnp.int32, (1, 128), 1)

    def emit_top(at, lane, value):
        f_out[at:at + 1, :] = jnp.where(lane2 >= lane, value, 0.0)

    def emit_bottom(at, lane, value):
        f_out[at:at + 1, 128:256] = jnp.where(lane1 >= lane, value, 0.0)

    top = []
    for p in range(16):
        a = g_ref[p * 8:p * 8 + 8, :] * scale
        b = g_ref[128 + p * 8:128 + p * 8 + 8, :] * scale
        top.append(jnp.concatenate([a, b], axis=1))
    f_out[128:256, 0:128] = jnp.zeros((128, 128), F32)
    factor_block(top, None, 2, 0, emit_top)
    side = f_out[0:128, 128:256]
    rest = g_ref[256:384, :] * scale - lax.dot_general(
        side, side, (((0,), (0,)), ((), ())), precision=lax.Precision.HIGHEST, preferred_element_type=F32
    )
    factor_block([rest[p * 8:p * 8 + 8, :] for p in range(16)], None, 1, 128, emit_bottom)
    cp.wait()


def body(slab, buckets, signs, counts):
    owners = lax.axis_size("rows")
    capacity = slab.shape[1] // owners
    width = slab.shape[2]
    place = lax.broadcasted_iota(jnp.int32, (owners, capacity), 1)
    weight = jnp.where(place < counts.reshape(owners, 1), signs.reshape(owners, capacity), 0)
    meta = jnp.concatenate([buckets.reshape(NZ, 64), weight.reshape(NZ, 64)], axis=1)
    vm = pl.BlockSpec(memory_space=pltpu.VMEM)
    anyspace = pl.BlockSpec(memory_space=pl.ANY)
    dma = pltpu.SemaphoreType.DMA
    sketch, gram = pl.pallas_call(
        gram_kernel,
        out_shape=(jax.ShapeDtypeStruct((BPO, width), F32), jax.ShapeDtypeStruct((384, 128), F32)),
        in_specs=[anyspace, vm],
        out_specs=(vm, vm),
        scratch_shapes=[
            pltpu.VMEM((8, 8, 8, 128), F32),
            pltpu.VMEM((8, 8, 8, 128), F32),
            pltpu.VMEM((8, 8, 8, 128), F32),
            pltpu.VMEM((8, 8, 8, 128), F32),
            pltpu.VMEM((8, 128), jnp.int32),
            pltpu.VMEM((2, 8, 8, 128), jnp.int32),
            pltpu.VMEM((128, 128), jnp.int32),
            pltpu.VMEM((384, 128), F32),
            pltpu.VMEM((192, 128), F32),
            pltpu.VMEM((192, 128), F32),
            pltpu.VMEM((8, 24, 128), F32),
            pltpu.VMEM((24, 128), F32),
            pltpu.VMEM((8, 8, 128), F32),
            pltpu.VMEM((8, 128), F32),
            pltpu.VMEM((4, 8, 128), F32),
            pltpu.VMEM((24, 128), F32),
            pltpu.VMEM((384, 128), F32),
            dma((5,)),
            dma((8,)), dma((8,)), dma((8,)), dma((8,)), dma((8,)), dma((8,)),
            dma((16,)), dma((16,)), dma((16,)), dma((16,)), dma((16,)), dma((16,)),
            dma, dma, dma((8,)), dma((8,)), dma((8,)), dma((8,)), dma((4,)), dma((4,)),
            dma((8,)), dma((8,)), dma((8,)), dma((8,)), dma((8,)), dma((8,)),
        ],
        compiler_params=pltpu.CompilerParams(
            collective_id=0, has_side_effects=True, vmem_limit_bytes=32 * 1024 * 1024
        ),
    )(slab.reshape(8, 8, 8, width), meta)
    slots = float(lax.axis_size("grp") * owners * owners * capacity)
    factor, sketch = pl.pallas_call(
        lambda *refs: factor_kernel(1.0 / slots, *refs),
        out_shape=(jax.ShapeDtypeStruct((width, width), F32), jax.ShapeDtypeStruct((BPO, width), F32)),
        in_specs=[vm, anyspace],
        out_specs=(vm, anyspace),
        scratch_shapes=[pltpu.SemaphoreType.DMA],
        compiler_params=pltpu.CompilerParams(vmem_limit_bytes=32 * 1024 * 1024),
    )(gram, sketch)
    return (sketch.reshape(1, BPO, width), factor)


def solution(mesh):
    in_specs = (P("grp", "rows", None), P("grp", "rows"), P("grp", "rows"), P("grp", "rows"))
    out_specs = (P("grp", "rows", None), P())
    return jax.shard_map(body, mesh=mesh, in_specs=in_specs, out_specs=out_specs, check_vma=False)
```

time: 408 us -> 76.1 us (0.19)
  waiting for transfers between devices: 306 us -> 0 us
  Pallas kernels: 0 us -> 71 us
  other arithmetic: 41.3 us -> 2.08 us
  starting transfers between devices: 35.8 us -> 0 us
  between operations: 15.5 us -> 0.69 us
  local copies, waits for them, and re-layouts: 6.48 us -> 2.17 us
    psum x1 -> x0, waiting for transfers between devices: 260 us -> none  [body(): gram = lax.psum(local_gram, ('rows', 'grp'))]
    pallas_call x0 -> x2, Pallas kernels: none -> 71 us  [the longest x1 60.2 us: body(): pl.pallas_call(gram_kernel, out_shape=(jax.ShapeDtypeStruct((BPO, width),...]
    all_to_all x4 -> x0, waiting for transfers between devices: 45.6 us -> none  [the longest x1 17 us: body(): lax.all_to_all(blocks, 'rows', split_axis=0, concat_axis=0, tiled=True)]
    all_to_all x4 -> x0, starting transfers between devices: 35.6 us -> none  [the longest x1 18.4 us: body(): lax.all_to_all(used_counts, 'rows', split_axis=0, concat_axis=0, tiled=True)]
    another operation x6 -> x0, other arithmetic: 34 us -> none  [body(): factor = jnp.linalg.cholesky(gram / total_slots).T]
  transfers between devices with their start and end apart: 5 -> 0, of which waited for: 5 -> 0; matrix products, arithmetic and copies ran while one was open for 2% -> 0% of each run, Pallas kernels for 0% -> 0%
where the time goes in v1:
time: 76.1 us; the launch traced here: 75.9 us
  Pallas kernels  71 us (93%)
  local copies, waits for them, and re-layouts  2.17 us (3%)
  other arithmetic  2.08 us (3%)
    pallas_call x1, Pallas kernels, body(): pl.pallas_call(gram_kernel, out_shape=(jax.ShapeDtypeStruct((BPO, width),...  60.2 us
    pallas_call x1, Pallas kernels, body(): pl.pallas_call(lambda *refs: factor_kernel(1.0 / slots, *refs), out_shape...  10.7 us
    unnamed x3, other arithmetic  2 us
    unnamed x9, local copies, waits for them, and re-layouts  1.7 us

profile of v1, /device:TPU:1, one launch (start us, length us, event | category | flops | bytes accessed | tf_op | source)
XLA Modules:
  0.0 75.9 jit_solution(12532795049419724996)
XLA Ops:
  0.6 0.0 copy-start.3
  0.6 0.0 copy-start.1
  0.6 0.5 broadcast.14
  1.2 0.1 copy-done.3
  1.3 0.7 reduce.10
  1.9 0.0 copy-done.1
  2.0 0.0 copy-start.2
  2.0 0.7 reduce.11
  2.6 0.0 copy-done.2
  2.6 0.7 reduce.9
  3.3 0.1 reshape.26
  3.4 0.1 reshape.25
  3.5 0.1 lt.13
  3.5 0.1 copy.6
  3.6 0.1 iota.12
  3.7 0.1 copy.7
  3.8 0.1 pad_add_fusion.meta
  3.9 0.0 copy-start
  3.9 1.1 %copy-done = f32[1,512,256]{2,1,0:T(8,128)S(1)} copy-done((f32[1,512,256]{2,1,0:T(8,128)S(1)}, f32[1,512,256]{2,1,0:T(8,128)}, u32[]{:S(2)}) %copy-start) | copy-done | bytes 524312
  4.9 60.2 %shard_map.59 = (f32[256,256]{1,0:T(8,128)S(1)}, f32[384,128]{1,0:T(8,128)S(1)}) custom-call(f32[8,8,8,256]{3,2,1,0:T(8,128)S(1)} %bitcast.3, s32[8,128]{1,0:T(8,128)S(1)} %pad_add_fusion.meta), custom_call_target="tpu_custom_call" | custom-call | tf_op jit(solution)/shard_map/pallas_call | solution.py:304
  65.2 10.7 %shard_map.60 = (f32[256,256]{1,0:T(8,128)}, f32[256,256]{1,0:T(8,128)}) custom-call(f32[384,128]{1,0:T(8,128)S(1)} %get-tuple-element.6.refs_0_, f32[256,256]{1,0:T(8,128)S(1)} %get-tuple-element.7.refs_1_), custom_call_target="tpu_custom_call" | custom-call | tf_op jit(solution)/shard_map/pallas_call | solution.py:338
  (3 shorter events, 0.0 us)
Async XLA Ops:
  0.6 0.7 copy-start.3
  0.6 1.3 %copy-start.1 = (s32[1,512]{1,0:T(1,128)S(1)}, s32[1,512]{1,0:T(1,128)}, u32[]{:S(2)}) copy-start(s32[1,512]{1,0:T(1,128)} %param.5) | copy-start | bytes 6148
  2.0 0.7 copy-start.2
  3.9 1.1 %copy-start = (f32[1,512,256]{2,1,0:T(8,128)S(1)}, f32[1,512,256]{2,1,0:T(8,128)}, u32[]{:S(2)}) copy-start(f32[1,512,256]{2,1,0:T(8,128)} %param.4) | copy-start | bytes 1572868

commit v2 on v1

v2 whole, which is shorter than its diff:
```python
import jax
import jax.numpy as jnp
from jax import lax
from jax.experimental import pallas as pl
from jax.experimental.pallas import tpu as pltpu
from jax.sharding import PartitionSpec as P

NZ = 8
NY = 8
NX = 4
BPO = 256
HALF = 128
F32 = jnp.float32
BF16 = jnp.bfloat16
MESH = pl.DeviceIdType.MESH
ORDER = (4, 3, 5, 2, 6, 1, 7)


def gram_kernel(
    slab_hbm, buckets_hbm, signs_hbm, counts_hbm, sk_out, g_out,
    slab, buckets, signs, counts, sk, meta, r1a, r1b, r2a, r2b, m1, m2, mt, gp, gx, acc, gz, part, gy, fin, gfull,
    loc_sem, s1a_s, s1a_r, s1b_s, s1b_r, s1m_s, s1m_r, s2a_s, s2a_r, s2b_s, s2b_r, s2m_s, s2m_r,
    x_s, x_r, z_s, z_r, y_s, y_r, zg_s, zg_r, xg_s, xg_r,
):
    r = lax.axis_index("rows")
    x = lax.axis_index("grp")
    z = r // 16
    y = (r // 2) % 8
    c = r % 2

    def dev(zz, yy, cc, xx):
        return ((zz * NY + yy) * 2 + cc, xx)

    barrier = pltpu.get_barrier_semaphore()
    peers = [dev(z, y, 1 - c, x)]
    for d in range(1, 8):
        for dc in range(2):
            peers.append(dev((z + d) % NZ, y, (c + dc) % 2, x))
            peers.append(dev(z, (y + d) % NY, (c + dc) % 2, x))
    for d in range(1, 4):
        for dc in range(2):
            peers.append(dev(z, y, (c + dc) % 2, (x + d) % NX))
    for p in peers:
        pl.semaphore_signal(barrier, inc=1, device_id=p, device_id_type=MESH)

    sends = []

    def rcopy(src, dst, ss, rs, to):
        cp = pltpu.make_async_remote_copy(
            src_ref=src, dst_ref=dst, send_sem=ss, recv_sem=rs, device_id=to, device_id_type=MESH
        )
        cp.start()
        sends.append(cp)
        return cp

    def lcopy(src, dst, sem):
        cp = pltpu.make_async_copy(src, dst, sem)
        cp.start()
        return cp

    load = lcopy(slab_hbm, slab, loc_sem.at[2])
    small = [
        lcopy(counts_hbm, counts, loc_sem.at[5]),
        lcopy(signs_hbm, signs, loc_sem.at[6]),
        lcopy(buckets_hbm, buckets, loc_sem.at[7]),
    ]
    slot = lax.broadcasted_iota(jnp.int32, (HALF, 512), 1)
    pair = lax.broadcasted_iota(jnp.int32, (HALF, 512), 0)
    spread = jnp.where(slot // 4 == pair, 1.0, 0.0).astype(BF16)
    for cp in small:
        cp.wait()
    limit = jnp.dot(
        jnp.broadcast_to(counts[...], (8, HALF)).astype(F32).astype(BF16), spread, preferred_element_type=F32
    )[0:1, :]
    place = lax.broadcasted_iota(jnp.int32, (1, 512), 1) % 4
    weight = jnp.where(place.astype(F32) < limit, signs[...], 0)
    for t in range(NZ):
        meta[t:t + 1, 0:64] = buckets[0:1, t * 64:t * 64 + 64]
        meta[t:t + 1, 64:128] = weight[0:1, t * 64:t * 64 + 64]
    load.wait()
    la = lcopy(slab.at[z, :, :, pl.ds(0, HALF)], r1a.at[z], loc_sem.at[0])
    lb = lcopy(slab.at[:, y, :, pl.ds(HALF, HALF)], r1b.at[y], loc_sem.at[1])
    m1[pl.ds(z, 1), :] = meta[pl.ds(z, 1), :]
    pl.semaphore_wait(barrier, len(peers))

    in_m, in_a, in_b = [], [], []
    for d in ORDER:
        zt = (z + d) % NZ
        in_m.append(rcopy(meta.at[pl.ds(zt, 1)], m1.at[pl.ds(z, 1)], s1m_s.at[d], s1m_r.at[d], dev(zt, y, c, x)))
    for d in ORDER:
        zt = (z + d) % NZ
        yt = (y + d) % NY
        in_a.append(rcopy(slab.at[zt, :, :, pl.ds(0, HALF)], r1a.at[z], s1a_s.at[d], s1a_r.at[d], dev(zt, y, c, x)))
        in_b.append(rcopy(slab.at[:, yt, :, pl.ds(HALF, HALF)], r1b.at[y], s1b_s.at[d], s1b_r.at[d], dev(z, yt, c, x)))

    for cp in in_m:
        cp.wait_recv()
    arrive = []
    for d in ORDER + (0,):
        for dc in range(2):
            if d == 0 and dc == 0:
                continue
            to = dev(z, (y + d) % NY, (c + dc) % 2, x)
            arrive.append(rcopy(m1, m2.at[c, y], s2m_s.at[d * 2 + dc], s2m_r.at[d * 2 + dc], to))
    m2[c, y] = m1[...]

    la.wait()
    for cp in in_a:
        cp.wait_recv()
    for d in ORDER + (0,):
        for dc in range(2):
            if d == 0 and dc == 0:
                continue
            yt = (y + d) % NY
            ct = (c + dc) % 2
            arrive.append(rcopy(
                r1a.at[:, yt, pl.ds(ct * 4, 4), :], r2a.at[y, :, pl.ds(c * 4, 4), :],
                s2a_s.at[d * 2 + dc], s2a_r.at[d * 2 + dc], dev(z, yt, ct, x),
            ))
    l2a = lcopy(r1a.at[:, y, pl.ds(c * 4, 4), :], r2a.at[y, :, pl.ds(c * 4, 4), :], loc_sem.at[3])
    lb.wait()
    for cp in in_b:
        cp.wait_recv()
    for d in ORDER + (0,):
        for dc in range(2):
            if d == 0 and dc == 0:
                continue
            zt = (z + d) % NZ
            ct = (c + dc) % 2
            arrive.append(rcopy(
                r1b.at[:, zt, pl.ds(ct * 4, 4), :], r2b.at[:, z, pl.ds(c * 4, 4), :],
                s2b_s.at[d * 2 + dc], s2b_r.at[d * 2 + dc], dev(zt, y, ct, x),
            ))
    l2b = lcopy(r1b.at[:, z, pl.ds(c * 4, 4), :], r2b.at[:, z, pl.ds(c * 4, 4), :], loc_sem.at[4])

    n_m = 15
    for cp in arrive[:n_m]:
        cp.wait_recv()
    mt[...] = jnp.transpose(m2[...].reshape(128, 128))
    b4 = mt[pl.ds(y * 8 + c * 4, 4), :]
    w4 = mt[pl.ds(64 + y * 8 + c * 4, 4), :]
    row = lax.broadcasted_iota(jnp.int32, (BPO, 128), 0)
    onehot = jnp.concatenate(
        [jnp.where(row == b4[s:s + 1, :], w4[s:s + 1, :], 0).astype(F32) for s in range(4)], axis=1
    ).astype(BF16)

    for cp in arrive[n_m:]:
        cp.wait_recv()
    l2a.wait()
    l2b.wait()
    fa = r2a.reshape(512, 128)
    fb = r2b.reshape(512, 128)
    rows = jnp.concatenate(
        [
            jnp.concatenate([f[pl.ds(k * 4 + s, 64, stride=8), :] for s in range(4) for k in range(2)], axis=0)
            for f in (fa, fb)
        ],
        axis=1,
    )
    hi = rows.astype(BF16)
    rest = rows - hi.astype(F32)
    mid = rest.astype(BF16)
    low = (rest - mid.astype(F32)).astype(BF16)
    sketch = jnp.dot(onehot, low, preferred_element_type=F32)
    sketch = sketch + jnp.dot(onehot, mid, preferred_element_type=F32)
    sketch = sketch + jnp.dot(onehot, hi, preferred_element_type=F32)
    sk[...] = sketch
    save = lcopy(sk, sk_out, loc_sem.at[8])

    def outer(a, b):
        return lax.dot_general(
            a, b, (((0,), (0,)), ((), ())), precision=lax.Precision.HIGHEST, preferred_element_type=F32
        )

    left = sketch[:, :HALF]
    right = sketch[:, HALF:]
    gp[pl.ds(0, 128), :] = outer(left, left)
    gp[pl.ds(128, 128), :] = outer(left, right)
    gp[pl.ds(256, 128), :] = outer(right, right)

    e = x * 2 + c
    near = [(d, dc) for d in (2, 1, 3, 0) for dc in range(2) if d or dc]
    got = []
    for d, dc in near:
        xt, ct = (x + d) % NX, (c + dc) % 2
        at = pl.ds((xt * 2 + ct) * 48, 48)
        got.append(rcopy(gp.at[at], gx.at[d * 2 + dc], x_s.at[d * 2 + dc], x_r.at[d * 2 + dc], dev(z, y, ct, xt)))
    total = gp[pl.ds(pl.multiple_of(e * 48, 8), 48), :]
    for (d, dc), cp in reversed(list(zip(near, got))):
        cp.wait_recv()
        total = total + gx[d * 2 + dc]
    acc[...] = total

    got = []
    for d in ORDER:
        zt = (z + d) % NZ
        got.append(rcopy(acc.at[pl.ds(zt * 6, 6)], gz.at[d, pl.ds(0, 6)], z_s.at[d], z_r.at[d], dev(zt, y, c, x)))
    total = acc[pl.ds(z * 6, 6), :]
    for d, cp in reversed(list(zip(ORDER, got))):
        cp.wait_recv()
        total = total + gz[d, 0:6]
    part[0:6, :] = total

    got = []
    for d in ORDER:
        yt = (y + d) % NY
        got.append(rcopy(part.at[pl.ds(0, 6)], gy.at[y, pl.ds(0, 6)], y_s.at[d], y_r.at[d], dev(z, yt, c, x)))
    gy[y, 0:6] = total
    for cp in got:
        cp.wait_recv()
    quad = [gy[2 * i, 0:6] + gy[2 * i + 1, 0:6] for i in range(4)]
    fin[pl.ds(z * 6, 6), :] = (quad[0] + quad[1]) + (quad[2] + quad[3])

    got = []
    mine = fin.at[pl.ds(z * 6, 6)]
    for d in ORDER:
        zt = (z + d) % NZ
        got.append(rcopy(mine, mine, zg_s.at[d], zg_r.at[d], dev(zt, y, c, x)))
    for cp in got:
        cp.wait_recv()

    got = []
    for d, dc in near:
        xt, ct = (x + d) % NX, (c + dc) % 2
        got.append(
            rcopy(fin, gfull.at[pl.ds(e * 48, 48)], xg_s.at[d * 2 + dc], xg_r.at[d * 2 + dc], dev(z, y, ct, xt))
        )
    gfull[pl.ds(pl.multiple_of(e * 48, 8), 48), :] = fin[...]
    for cp in got:
        cp.wait_recv()
    g_out[...] = gfull[...]
    save.wait()
    for cp in sends:
        cp.wait_send()


def splat(v):
    return jnp.broadcast_to(v, (8, HALF))


def recip(v):
    guess = pl.reciprocal(v, approx=True)
    guess = guess * (2.0 - v * guess)
    return guess * (2.0 - v * guess)


def factor_block(groups, k0, emit):
    n = len(groups)
    tiles = len(groups[0])
    for p in range(n):
        base = p * 8
        lead = groups[p]
        ahead = p + 1 < n
        column = [splat(lead[0][:, base + j:base + j + 1]) for j in range(8)]
        d = [[splat(column[j][i:i + 1, :]) for j in range(i + 1)] for i in range(8)]
        rows = [[splat(t[i:i + 1, :]) for t in lead] for i in range(8)]
        if ahead:
            nxt = list(groups[p + 1])
            side = [splat(nxt[0][:, base + j:base + j + 1]) for j in range(8)]
        final = []
        for b in range(0, 8, 2):
            p00, p10, p11 = d[b][b], d[b + 1][b], d[b + 1][b + 1]
            inv = recip(p00 * p11 - p10 * p10)
            x0, x1 = rows[b], rows[b + 1]
            if ahead:
                m0 = (p11 * side[b] - p10 * side[b + 1]) * inv
                m1 = (p00 * side[b + 1] - p10 * side[b]) * inv
                nxt = [t - (m0 * x0[k] + m1 * x1[k]) for k, t in enumerate(nxt)]
                for i in range(b + 2, 8):
                    side[i] = side[i] - (m0 * d[i][b] + m1 * d[i][b + 1])
            for i in range(b + 2, 8):
                n0 = p11 * d[i][b] - p10 * d[i][b + 1]
                n1 = p00 * d[i][b + 1] - p10 * d[i][b]
                for j in range(b + 2, i + 1):
                    d[i][j] = d[i][j] - (n0 * d[j][b] + n1 * d[j][b + 1]) * inv
                n0, n1 = n0 * inv, n1 * inv
                rows[i] = [t - (n0 * x0[k] + n1 * x1[k]) for k, t in enumerate(rows[i])]
            r0 = lax.rsqrt(p00)
            low = p10 * r0
            r1 = lax.rsqrt(p11 - low * low)
            first = [t * r0 for t in x0]
            final.append(first)
            final.append([(t - low * first[k]) * r1 for k, t in enumerate(x1)])
        for j in range(8):
            emit(k0 + base + j, base + j, [t[0:1, :] for t in final[j]])
        if ahead:
            groups[p + 1] = nxt
        if p + 2 < n:
            panel = jnp.concatenate([final[j][0][0:1, :] for j in range(8)], axis=0)
            turned = jnp.transpose(panel)
            for g in range(p + 2, n):
                mult = [splat(turned[g * 8:g * 8 + 8, j:j + 1]) for j in range(8)]
                for k in range(tiles):
                    terms = [mult[j] * final[j][k] for j in range(8)]
                    while len(terms) > 1:
                        terms = [terms[i] + terms[i + 1] for i in range(0, len(terms), 2)]
                    groups[g][k] = groups[g][k] - terms[0]


def factor_kernel(scale, g_ref, sk_ref, f_out, sk_out, sem):
    cp = pltpu.make_async_copy(sk_ref, sk_out, sem)
    cp.start()
    lane = lax.broadcasted_iota(jnp.int32, (8, HALF), 1)
    sub = lax.broadcasted_iota(jnp.int32, (8, HALF), 0)
    across, down = [], []
    for at in (0, 256):
        picked = [jnp.where(lane == sub + p * 8, g_ref[at + p * 8:at + p * 8 + 8, :], 0.0) for p in range(16)]
        down.append([lax.rsqrt(splat(jnp.sum(t, axis=1, keepdims=True))) for t in picked])
        while len(picked) > 1:
            picked = [picked[i] + picked[i + 1] for i in range(0, len(picked), 2)]
        across.append(splat(jnp.sum(picked[0], axis=0, keepdims=True)))
    scaled = [lax.rsqrt(v) for v in across]
    back = [jnp.sqrt(v * scale) for v in across]

    def emit(first):
        def put(at, diagonal, values):
            for k, v in enumerate(values):
                v = v * back[first + k][0:1, :]
                if k == 0:
                    v = jnp.where(lane[0:1, :] >= diagonal, v, 0.0)
                f_out[at:at + 1, (first + k) * HALF:(first + k + 1) * HALF] = v
                if keep is not None and k == 1:
                    keep.append(values[1])
        return put

    keep = []
    top = []
    for p in range(16):
        top.append([
            g_ref[p * 8:p * 8 + 8, :] * (down[0][p] * scaled[0]),
            g_ref[128 + p * 8:128 + p * 8 + 8, :] * (down[0][p] * scaled[1]),
        ])
    f_out[128:256, 0:128] = jnp.zeros((128, 128), F32)
    factor_block(top, 0, emit(0))
    corner = jnp.concatenate(keep, axis=0)
    keep = None
    less = lax.dot_general(
        corner, corner, (((0,), (0,)), ((), ())), precision=lax.Precision.HIGHEST, preferred_element_type=F32
    )
    bottom = []
    for p in range(16):
        at = 256 + p * 8
        bottom.append([g_ref[at:at + 8, :] * (down[1][p] * scaled[1]) - less[p * 8:p * 8 + 8, :]])
    factor_block(bottom, 128, emit(1))
    cp.wait()


def body(slab, buckets, signs, counts):
    owners = lax.axis_size("rows")
    capacity = slab.shape[1] // owners
    width = slab.shape[2]
    vm = pl.BlockSpec(memory_space=pltpu.VMEM)
    hbm = pl.BlockSpec(memory_space=pltpu.HBM)
    dma = pltpu.SemaphoreType.DMA
    sketch, gram = pl.pallas_call(
        gram_kernel,
        out_shape=(jax.ShapeDtypeStruct((BPO, width), F32), jax.ShapeDtypeStruct((384, 128), F32)),
        in_specs=[hbm] * 4,
        out_specs=(hbm, vm),
        scratch_shapes=[
            pltpu.VMEM((8, 8, 8, 256), F32),
            pltpu.VMEM((1, 512), jnp.int32),
            pltpu.VMEM((1, 512), jnp.int32),
            pltpu.VMEM((1, 128), jnp.int32),
            pltpu.VMEM((256, 256), F32),
            pltpu.VMEM((8, 128), jnp.int32),
            pltpu.VMEM((8, 8, 8, 128), F32),
            pltpu.VMEM((8, 8, 8, 128), F32),
            pltpu.VMEM((8, 8, 8, 128), F32),
            pltpu.VMEM((8, 8, 8, 128), F32),
            pltpu.VMEM((8, 128), jnp.int32),
            pltpu.VMEM((2, 8, 8, 128), jnp.int32),
            pltpu.VMEM((128, 128), jnp.int32),
            pltpu.VMEM((384, 128), F32),
            pltpu.VMEM((8, 48, 128), F32),
            pltpu.VMEM((48, 128), F32),
            pltpu.VMEM((8, 8, 128), F32),
            pltpu.VMEM((8, 128), F32),
            pltpu.VMEM((8, 8, 128), F32),
            pltpu.VMEM((48, 128), F32),
            pltpu.VMEM((384, 128), F32),
            dma((9,)),
            dma((8,)), dma((8,)), dma((8,)), dma((8,)), dma((8,)), dma((8,)),
            dma((16,)), dma((16,)), dma((16,)), dma((16,)), dma((16,)), dma((16,)),
            dma((8,)), dma((8,)), dma((8,)), dma((8,)), dma((8,)), dma((8,)),
            dma((8,)), dma((8,)), dma((8,)), dma((8,)),
        ],
        compiler_params=pltpu.CompilerParams(
            collective_id=0, has_side_effects=True, vmem_limit_bytes=60 * 1024 * 1024
        ),
    )(slab.reshape(8, 8, 8, width), buckets, signs, counts)
    slots = float(lax.axis_size("grp") * owners * owners * capacity)
    factor, sketch = pl.pallas_call(
        lambda *refs: factor_kernel(1.0 / slots, *refs),
        out_shape=(jax.ShapeDtypeStruct((width, width), F32), jax.ShapeDtypeStruct((BPO, width), F32)),
        in_specs=[vm, hbm],
        out_specs=(vm, hbm),
        scratch_shapes=[pltpu.SemaphoreType.DMA],
        compiler_params=pltpu.CompilerParams(vmem_limit_bytes=60 * 1024 * 1024),
    )(gram, sketch)
    return (sketch.reshape(1, BPO, width), factor)


def solution(mesh):
    in_specs = (P("grp", "rows", None), P("grp", "rows"), P("grp", "rows"), P("grp", "rows"))
    out_specs = (P("grp", "rows", None), P())
    return jax.shard_map(body, mesh=mesh, in_specs=in_specs, out_specs=out_specs, check_vma=False)
```

time: 76.1 us -> 70.4 us (0.925)
  local copies, waits for them, and re-layouts: 2.17 us -> 0 us
  other arithmetic: 2.08 us -> 0 us
  Pallas kernels: 71 us -> 69.6 us
    pallas_call x1, Pallas kernels: 60.2 us -> 57.6 us  [body(): pl.pallas_call(gram_kernel, out_shape=(jax.ShapeDtypeStruct((BPO, width),...]
    unnamed x3 -> x0, other arithmetic: 2 us -> none
    unnamed x9 -> x0, local copies, waits for them, and re-layouts: 1.7 us -> none
    pallas_call x1, Pallas kernels: 10.7 us -> 12 us  [body(): pl.pallas_call(lambda *refs: factor_kernel(1.0 / slots, *refs), out_shape...]
where the time goes in v2:
time: 70.4 us; the launch traced here: 70.3 us
  Pallas kernels  69.6 us (99%)
    pallas_call x1, Pallas kernels, body(): pl.pallas_call(gram_kernel, out_shape=(jax.ShapeDtypeStruct((BPO, width),...  57.6 us
    pallas_call x1, Pallas kernels, body(): pl.pallas_call(lambda *refs: factor_kernel(1.0 / slots, *refs), out_shape...  12 us

profile of v2, /device:TPU:1, one launch (start us, length us, event | category | flops | bytes accessed | tf_op | source)
XLA Modules:
  0.0 70.3 jit_solution(12481664022423953519)
XLA Ops:
  0.6 57.6 %shard_map.59 = (f32[256,256]{1,0:T(8,128)}, f32[384,128]{1,0:T(8,128)}) custom-call(f32[8,8,8,256]{3,2,1,0:T(8,128)} %bitcast.2, s32[1,512]{1,0:T(1,128)} %buckets_hbm.1, s32[1,512]{1,0:T(1,128)} %signs_hbm.1, s32[1,128]{1,0:T(1,128)} %counts_hbm.1), custom_call_target="tpu_custom_call" | custom-call | tf_op jit(solution)/shard_map/pallas_call | solution.py:355
  58.3 12.0 %shard_map.60 = (f32[256,256]{1,0:T(8,128)}, f32[256,256]{1,0:T(8,128)}) custom-call(f32[384,128]{1,0:T(8,128)} %get-tuple-element.6.refs_0_, f32[256,256]{1,0:T(8,128)} %get-tuple-element.7.refs_1_), custom_call_target="tpu_custom_call" | custom-call | tf_op jit(solution)/shard_map/pallas_call | solution.py:393

commit v3 on v2

--- a/solution.py
+++ b/solution.py
@@ -18,8 +18,8 @@
 
 def gram_kernel(
     slab_hbm, buckets_hbm, signs_hbm, counts_hbm, sk_out, g_out,
-    slab, buckets, signs, counts, sk, meta, r1a, r1b, r2a, r2b, m1, m2, mt, gp, gx, acc, gz, part, gy, fin, gfull,
-    loc_sem, s1a_s, s1a_r, s1b_s, s1b_r, s1m_s, s1m_r, s2a_s, s2a_r, s2b_s, s2b_r, s2m_s, s2m_r,
+    ha, hb, buckets, signs, counts, sk, out1, r1a, r1b, r2a, r2b, mt, gp, gx, acc, gz, part, gy, fin, gfull,
+    loc_sem, s1a_s, s1a_r, s1b_s, s1b_r, s2a_s, s2a_r, s2b_s, s2b_r,
     x_s, x_r, z_s, z_r, y_s, y_r, zg_s, zg_r, xg_s, xg_r,
 ):
     r = lax.axis_index("rows")
@@ -58,51 +58,43 @@
         cp.start()
         return cp
 
-    load = lcopy(slab_hbm, slab, loc_sem.at[2])
+    load = lcopy(slab_hbm.at[:, :, :, pl.ds(0, HALF)], ha, loc_sem.at[2])
+    load_b = lcopy(slab_hbm.at[:, :, :, pl.ds(HALF, HALF)], hb, loc_sem.at[9])
     small = [
         lcopy(counts_hbm, counts, loc_sem.at[5]),
         lcopy(signs_hbm, signs, loc_sem.at[6]),
         lcopy(buckets_hbm, buckets, loc_sem.at[7]),
     ]
-    slot = lax.broadcasted_iota(jnp.int32, (HALF, 512), 1)
-    pair = lax.broadcasted_iota(jnp.int32, (HALF, 512), 0)
-    spread = jnp.where(slot // 4 == pair, 1.0, 0.0).astype(BF16)
     for cp in small:
         cp.wait()
-    limit = jnp.dot(
-        jnp.broadcast_to(counts[...], (8, HALF)).astype(F32).astype(BF16), spread, preferred_element_type=F32
-    )[0:1, :]
-    place = lax.broadcasted_iota(jnp.int32, (1, 512), 1) % 4
-    weight = jnp.where(place.astype(F32) < limit, signs[...], 0)
-    for t in range(NZ):
-        meta[t:t + 1, 0:64] = buckets[0:1, t * 64:t * 64 + 64]
-        meta[t:t + 1, 64:128] = weight[0:1, t * 64:t * 64 + 64]
+
+    def fold(values, each, first):
+        count = values.shape[1]
+        at = lax.broadcasted_iota(jnp.int32, (64, count), 1)
+        pair = lax.broadcasted_iota(jnp.int32, (64, count), 0)
+        mine = jnp.where(at // each == pair, values[...], 0).astype(F32).astype(BF16)
+        src = lax.broadcasted_iota(jnp.int32, (count, HALF), 0)
+        dst = lax.broadcasted_iota(jnp.int32, (count, HALF), 1)
+        pick = jnp.where(src % each + first == dst, 1.0, 0.0).astype(BF16)
+        return jnp.dot(mine, pick, preferred_element_type=F32)
+
+    rows9 = out1.reshape(576, HALF)
+    rows9[pl.ds(4, 64, stride=9), :] = fold(buckets, 8, 0) + fold(signs, 8, 8) + fold(counts, 2, 16)
     load.wait()
-    la = lcopy(slab.at[z, :, :, pl.ds(0, HALF)], r1a.at[z], loc_sem.at[0])
-    lb = lcopy(slab.at[:, y, :, pl.ds(HALF, HALF)], r1b.at[y], loc_sem.at[1])
-    m1[pl.ds(z, 1), :] = meta[pl.ds(z, 1), :]
+    flat = ha.reshape(512, HALF)
+    for i in range(8):
+        rows9[pl.ds(i + i // 4, 64, stride=9), :] = flat[pl.ds(i, 64, stride=8), :]
+    load_b.wait()
+    la = lcopy(out1.at[z], r1a.at[z], loc_sem.at[0])
+    lb = lcopy(hb.at[:, y], r1b.at[y], loc_sem.at[1])
     pl.semaphore_wait(barrier, len(peers))
 
-    in_m, in_a, in_b = [], [], []
-    for d in ORDER:
-        zt = (z + d) % NZ
-        in_m.append(rcopy(meta.at[pl.ds(zt, 1)], m1.at[pl.ds(z, 1)], s1m_s.at[d], s1m_r.at[d], dev(zt, y, c, x)))
+    in_a, in_b, arrive = [], [], []
     for d in ORDER:
         zt = (z + d) % NZ
         yt = (y + d) % NY
-        in_a.append(rcopy(slab.at[zt, :, :, pl.ds(0, HALF)], r1a.at[z], s1a_s.at[d], s1a_r.at[d], dev(zt, y, c, x)))
-        in_b.append(rcopy(slab.at[:, yt, :, pl.ds(HALF, HALF)], r1b.at[y], s1b_s.at[d], s1b_r.at[d], dev(z, yt, c, x)))
-
-    for cp in in_m:
-        cp.wait_recv()
-    arrive = []
-    for d in ORDER + (0,):
-        for dc in range(2):
-            if d == 0 and dc == 0:
-                continue
-            to = dev(z, (y + d) % NY, (c + dc) % 2, x)
-            arrive.append(rcopy(m1, m2.at[c, y], s2m_s.at[d * 2 + dc], s2m_r.at[d * 2 + dc], to))
-    m2[c, y] = m1[...]
+        in_a.append(rcopy(out1.at[zt], r1a.at[z], s1a_s.at[d], s1a_r.at[d], dev(zt, y, c, x)))
+        in_b.append(rcopy(hb.at[:, yt], r1b.at[y], s1b_s.at[d], s1b_r.at[d], dev(z, yt, c, x)))
 
     la.wait()
     for cp in in_a:
@@ -114,10 +106,10 @@
             yt = (y + d) % NY
             ct = (c + dc) % 2
             arrive.append(rcopy(
-                r1a.at[:, yt, pl.ds(ct * 4, 4), :], r2a.at[y, :, pl.ds(c * 4, 4), :],
+                r1a.at[:, pl.ds(yt * 9 + ct * 4, 5), :], r2a.at[c, y, :, pl.ds(0, 5), :],
                 s2a_s.at[d * 2 + dc], s2a_r.at[d * 2 + dc], dev(z, yt, ct, x),
             ))
-    l2a = lcopy(r1a.at[:, y, pl.ds(c * 4, 4), :], r2a.at[y, :, pl.ds(c * 4, 4), :], loc_sem.at[3])
+    l2a = lcopy(r1a.at[:, pl.ds(y * 9 + c * 4, 5), :], r2a.at[c, y, :, pl.ds(0, 5), :], loc_sem.at[3])
     lb.wait()
     for cp in in_b:
         cp.wait_recv()
@@ -133,30 +125,28 @@
             ))
     l2b = lcopy(r1b.at[:, z, pl.ds(c * 4, 4), :], r2b.at[:, z, pl.ds(c * 4, 4), :], loc_sem.at[4])
 
-    n_m = 15
-    for cp in arrive[:n_m]:
-        cp.wait_recv()
-    mt[...] = jnp.transpose(m2[...].reshape(128, 128))
-    b4 = mt[pl.ds(y * 8 + c * 4, 4), :]
-    w4 = mt[pl.ds(64 + y * 8 + c * 4, 4), :]
-    row = lax.broadcasted_iota(jnp.int32, (BPO, 128), 0)
+    l2a.wait()
+    for cp in arrive[:15]:
+        cp.wait_recv()
+    fa = r2a.reshape(1024, HALF)
+    fb = r2b.reshape(512, HALF)
+    mt[...] = jnp.transpose(fa[pl.ds(4 - 4 * c, 128, stride=8), :])
+    b4 = mt[pl.ds(c * 4, 4), :]
+    s4 = mt[pl.ds(8 + c * 4, 4), :]
+    used = mt[pl.ds(16 + c, 1), :]
+    row = lax.broadcasted_iota(jnp.int32, (BPO, HALF), 0).astype(F32)
     onehot = jnp.concatenate(
-        [jnp.where(row == b4[s:s + 1, :], w4[s:s + 1, :], 0).astype(F32) for s in range(4)], axis=1
+        [jnp.where(row == b4[s:s + 1, :], jnp.where(used > s, s4[s:s + 1, :], 0.0), 0.0) for s in range(4)], axis=1
     ).astype(BF16)
-
-    for cp in arrive[n_m:]:
-        cp.wait_recv()
-    l2a.wait()
+    rows_a = jnp.concatenate([fa[pl.ds(s + c, 128, stride=8), :] for s in range(4)], axis=0)
+
     l2b.wait()
-    fa = r2a.reshape(512, 128)
-    fb = r2b.reshape(512, 128)
-    rows = jnp.concatenate(
-        [
-            jnp.concatenate([f[pl.ds(k * 4 + s, 64, stride=8), :] for s in range(4) for k in range(2)], axis=0)
-            for f in (fa, fb)
-        ],
-        axis=1,
+    for cp in arrive[15:]:
+        cp.wait_recv()
+    rows_b = jnp.concatenate(
+        [fb[pl.ds(k * 4 + s, 64, stride=8), :] for s in range(4) for k in range(2)], axis=0
     )
+    rows = jnp.concatenate([rows_a, rows_b], axis=1)
     hi = rows.astype(BF16)
     rest = rows - hi.astype(F32)
     mid = rest.astype(BF16)
@@ -167,16 +157,22 @@
     sk[...] = sketch
     save = lcopy(sk, sk_out, loc_sem.at[8])
 
-    def outer(a, b):
-        return lax.dot_general(
-            a, b, (((0,), (0,)), ((), ())), precision=lax.Precision.HIGHEST, preferred_element_type=F32
-        )
-
-    left = sketch[:, :HALF]
-    right = sketch[:, HALF:]
-    gp[pl.ds(0, 128), :] = outer(left, left)
-    gp[pl.ds(128, 128), :] = outer(left, right)
-    gp[pl.ds(256, 128), :] = outer(right, right)
+    turned = jnp.transpose(sketch)
+
+    def pieces(v):
+        first = v.astype(BF16)
+        v = v - first.astype(F32)
+        second = v.astype(BF16)
+        return first, second, (v - second.astype(F32)).astype(BF16)
+
+    ta, tb, tc = pieces(turned)
+    sa, sb, sc = pieces(sketch)
+    gram = jnp.zeros((BPO, BPO), F32)
+    for left, right in ((tc, sa), (ta, sc), (tb, sb), (tb, sa), (ta, sb), (ta, sa)):
+        gram = gram + jnp.dot(left, right, preferred_element_type=F32)
+    gp[pl.ds(0, 128), :] = gram[:HALF, :HALF]
+    gp[pl.ds(128, 128), :] = gram[:HALF, HALF:]
+    gp[pl.ds(256, 128), :] = gram[HALF:, HALF:]
 
     e = x * 2 + c
     near = [(d, dc) for d in (2, 1, 3, 0) for dc in range(2) if d or dc]
@@ -240,22 +236,19 @@
 
 def recip(v):
     guess = pl.reciprocal(v, approx=True)
-    guess = guess * (2.0 - v * guess)
     return guess * (2.0 - v * guess)
 
 
-def factor_block(groups, k0, emit):
-    n = len(groups)
-    tiles = len(groups[0])
+def factor_block(mats, k0, emit):
+    tiles = len(mats)
+    n = 16
     for p in range(n):
         base = p * 8
-        lead = groups[p]
         ahead = p + 1 < n
-        column = [splat(lead[0][:, base + j:base + j + 1]) for j in range(8)]
-        d = [[splat(column[j][i:i + 1, :]) for j in range(i + 1)] for i in range(8)]
-        rows = [[splat(t[i:i + 1, :]) for t in lead] for i in range(8)]
+        rows = [[m[pl.ds(base + i, 8, stride=0), :] for m in mats] for i in range(8)]
+        d = [[splat(rows[i][0][:, base + j:base + j + 1]) for j in range(i + 1)] for i in range(8)]
         if ahead:
-            nxt = list(groups[p + 1])
+            nxt = [m[base + 8:base + 16, :] for m in mats]
             side = [splat(nxt[0][:, base + j:base + j + 1]) for j in range(8)]
         final = []
         for b in range(0, 8, 2):
@@ -263,11 +256,13 @@
             inv = recip(p00 * p11 - p10 * p10)
             x0, x1 = rows[b], rows[b + 1]
             if ahead:
-                m0 = (p11 * side[b] - p10 * side[b + 1]) * inv
-                m1 = (p00 * side[b + 1] - p10 * side[b]) * inv
-                nxt = [t - (m0 * x0[k] + m1 * x1[k]) for k, t in enumerate(nxt)]
+                n0 = p11 * side[b] - p10 * side[b + 1]
+                n1 = p00 * side[b + 1] - p10 * side[b]
+                nxt = [t - (n0 * x0[k] + n1 * x1[k]) * inv for k, t in enumerate(nxt)]
+                if b < 6:
+                    n0, n1 = n0 * inv, n1 * inv
                 for i in range(b + 2, 8):
-                    side[i] = side[i] - (m0 * d[i][b] + m1 * d[i][b + 1])
+                    side[i] = side[i] - (n0 * d[i][b] + n1 * d[i][b + 1])
             for i in range(b + 2, 8):
                 n0 = p11 * d[i][b] - p10 * d[i][b + 1]
                 n1 = p00 * d[i][b + 1] - p10 * d[i][b]
@@ -281,23 +276,24 @@
             first = [t * r0 for t in x0]
             final.append(first)
             final.append([(t - low * first[k]) * r1 for k, t in enumerate(x1)])
+        if ahead:
+            for k, m in enumerate(mats):
+                m[base + 8:base + 16, :] = nxt[k]
         for j in range(8):
             emit(k0 + base + j, base + j, [t[0:1, :] for t in final[j]])
-        if ahead:
-            groups[p + 1] = nxt
         if p + 2 < n:
             panel = jnp.concatenate([final[j][0][0:1, :] for j in range(8)], axis=0)
             turned = jnp.transpose(panel)
             for g in range(p + 2, n):
                 mult = [splat(turned[g * 8:g * 8 + 8, j:j + 1]) for j in range(8)]
-                for k in range(tiles):
+                for k, m in enumerate(mats):
                     terms = [mult[j] * final[j][k] for j in range(8)]
                     while len(terms) > 1:
                         terms = [terms[i] + terms[i + 1] for i in range(0, len(terms), 2)]
-                    groups[g][k] = groups[g][k] - terms[0]
-
-
-def factor_kernel(scale, g_ref, sk_ref, f_out, sk_out, sem):
+                    m[g * 8:g * 8 + 8, :] = m[g * 8:g * 8 + 8, :] - terms[0]
+
+
+def factor_kernel(scale, g_ref, sk_ref, f_out, sk_out, a0, a1, sem):
     cp = pltpu.make_async_copy(sk_ref, sk_out, sem)
     cp.start()
     lane = lax.broadcasted_iota(jnp.int32, (8, HALF), 1)
@@ -319,29 +315,23 @@
                 if k == 0:
                     v = jnp.where(lane[0:1, :] >= diagonal, v, 0.0)
                 f_out[at:at + 1, (first + k) * HALF:(first + k + 1) * HALF] = v
-                if keep is not None and k == 1:
-                    keep.append(values[1])
         return put
 
-    keep = []
-    top = []
     for p in range(16):
-        top.append([
-            g_ref[p * 8:p * 8 + 8, :] * (down[0][p] * scaled[0]),
-            g_ref[128 + p * 8:128 + p * 8 + 8, :] * (down[0][p] * scaled[1]),
-        ])
+        at = p * 8
+        a0[at:at + 8, :] = g_ref[at:at + 8, :] * (down[0][p] * scaled[0])
+        a1[at:at + 8, :] = g_ref[128 + at:128 + at + 8, :] * (down[0][p] * scaled[1])
     f_out[128:256, 0:128] = jnp.zeros((128, 128), F32)
-    factor_block(top, 0, emit(0))
-    corner = jnp.concatenate(keep, axis=0)
-    keep = None
+    factor_block([a0, a1], 0, emit(0))
+    corner = f_out[0:128, 128:256]
     less = lax.dot_general(
         corner, corner, (((0,), (0,)), ((), ())), precision=lax.Precision.HIGHEST, preferred_element_type=F32
     )
-    bottom = []
     for p in range(16):
-        at = 256 + p * 8
-        bottom.append([g_ref[at:at + 8, :] * (down[1][p] * scaled[1]) - less[p * 8:p * 8 + 8, :]])
-    factor_block(bottom, 128, emit(1))
+        at = p * 8
+        left = g_ref[256 + at:256 + at + 8, :] - less[at:at + 8, :] * (1.0 / scale)
+        a0[at:at + 8, :] = left * (down[1][p] * scaled[1])
+    factor_block([a0], 128, emit(1))
     cp.wait()
 
 
@@ -358,19 +348,18 @@
         in_specs=[hbm] * 4,
         out_specs=(hbm, vm),
         scratch_shapes=[
-            pltpu.VMEM((8, 8, 8, 256), F32),
+            pltpu.VMEM((8, 8, 8, 128), F32),
+            pltpu.VMEM((8, 8, 8, 128), F32),
             pltpu.VMEM((1, 512), jnp.int32),
             pltpu.VMEM((1, 512), jnp.int32),
             pltpu.VMEM((1, 128), jnp.int32),
             pltpu.VMEM((256, 256), F32),
-            pltpu.VMEM((8, 128), jnp.int32),
+            pltpu.VMEM((8, 72, 128), F32),
+            pltpu.VMEM((8, 72, 128), F32),
             pltpu.VMEM((8, 8, 8, 128), F32),
+            pltpu.VMEM((2, 8, 8, 8, 128), F32),
             pltpu.VMEM((8, 8, 8, 128), F32),
-            pltpu.VMEM((8, 8, 8, 128), F32),
-            pltpu.VMEM((8, 8, 8, 128), F32),
-            pltpu.VMEM((8, 128), jnp.int32),
-            pltpu.VMEM((2, 8, 8, 128), jnp.int32),
-            pltpu.VMEM((128, 128), jnp.int32),
+            pltpu.VMEM((128, 128), F32),
             pltpu.VMEM((384, 128), F32),
             pltpu.VMEM((8, 48, 128), F32),
             pltpu.VMEM((48, 128), F32),
@@ -379,9 +368,9 @@
             pltpu.VMEM((8, 8, 128), F32),
             pltpu.VMEM((48, 128), F32),
             pltpu.VMEM((384, 128), F32),
-            dma((9,)),
-            dma((8,)), dma((8,)), dma((8,)), dma((8,)), dma((8,)), dma((8,)),
-            dma((16,)), dma((16,)), dma((16,)), dma((16,)), dma((16,)), dma((16,)),
+            dma((10,)),
+            dma((8,)), dma((8,)), dma((8,)), dma((8,)),
+            dma((16,)), dma((16,)), dma((16,)), dma((16,)),
             dma((8,)), dma((8,)), dma((8,)), dma((8,)), dma((8,)), dma((8,)),
             dma((8,)), dma((8,)), dma((8,)), dma((8,)),
         ],
@@ -395,7 +384,11 @@
         out_shape=(jax.ShapeDtypeStruct((width, width), F32), jax.ShapeDtypeStruct((BPO, width), F32)),
         in_specs=[vm, hbm],
         out_specs=(vm, hbm),
-        scratch_shapes=[pltpu.SemaphoreType.DMA],
+        scratch_shapes=[
+            pltpu.VMEM((HALF, HALF), F32),
+            pltpu.VMEM((HALF, HALF), F32),
+            pltpu.SemaphoreType.DMA,
+        ],
         compiler_params=pltpu.CompilerParams(vmem_limit_bytes=60 * 1024 * 1024),
     )(gram, sketch)
     return (sketch.reshape(1, BPO, width), factor)

time: 70.4 us -> 71.6 us (1.017)
  Pallas kernels: 69.6 us -> 70.8 us
    pallas_call x1, Pallas kernels: 57.6 us -> 58.8 us  [body(): pl.pallas_call(gram_kernel, out_shape=(jax.ShapeDtypeStruct((BPO, width),...]
where the time goes in v3:
time: 71.6 us; the launch traced here: 71.5 us
  Pallas kernels  70.8 us (99%)
    pallas_call x1, Pallas kernels, body(): pl.pallas_call(gram_kernel, out_shape=(jax.ShapeDtypeStruct((BPO, width),...  58.8 us
    pallas_call x1, Pallas kernels, body(): pl.pallas_call(lambda *refs: factor_kernel(1.0 / slots, *refs), out_shape...  12.1 us

profile of v3, /device:TPU:1, one launch (start us, length us, event | category | flops | bytes accessed | tf_op | source)
XLA Modules:
  0.0 71.5 jit_solution(15199696897394669724)
XLA Ops:
  0.6 58.8 %shard_map.59 = (f32[256,256]{1,0:T(8,128)}, f32[384,128]{1,0:T(8,128)}) custom-call(f32[8,8,8,256]{3,2,1,0:T(8,128)} %bitcast.2, s32[1,512]{1,0:T(1,128)} %buckets_hbm.1, s32[1,512]{1,0:T(1,128)} %signs_hbm.1, s32[1,128]{1,0:T(1,128)} %counts_hbm.1), custom_call_target="tpu_custom_call" | custom-call | tf_op jit(solution)/shard_map/pallas_call | solution.py:345
  59.4 12.1 %shard_map.60 = (f32[256,256]{1,0:T(8,128)}, f32[256,256]{1,0:T(8,128)}) custom-call(f32[384,128]{1,0:T(8,128)} %get-tuple-element.6.refs_0_, f32[256,256]{1,0:T(8,128)} %get-tuple-element.7.refs_1_), custom_call_target="tpu_custom_call" | custom-call | tf_op jit(solution)/shard_map/pallas_call | solution.py:382

commit v4 on v2

--- a/solution.py
+++ b/solution.py
@@ -78,20 +78,34 @@
         meta[t:t + 1, 0:64] = buckets[0:1, t * 64:t * 64 + 64]
         meta[t:t + 1, 64:128] = weight[0:1, t * 64:t * 64 + 64]
     load.wait()
-    la = lcopy(slab.at[z, :, :, pl.ds(0, HALF)], r1a.at[z], loc_sem.at[0])
-    lb = lcopy(slab.at[:, y, :, pl.ds(HALF, HALF)], r1b.at[y], loc_sem.at[1])
+    own = {}
+    for q in range(2):
+        yl, zl = (y + q) % 2, (z + q) % 2
+        own[q] = (
+            lcopy(slab.at[z // 2, z % 2, :, yl, :, pl.ds(0, HALF)], r1a.at[z, yl], loc_sem.at[9 + q]),
+            lcopy(slab.at[:, zl, y // 2, y % 2, :, pl.ds(HALF, HALF)], r1b.at[y, zl], loc_sem.at[11 + q]),
+        )
     m1[pl.ds(z, 1), :] = meta[pl.ds(z, 1), :]
     pl.semaphore_wait(barrier, len(peers))
 
-    in_m, in_a, in_b = [], [], []
+    in_m = []
     for d in ORDER:
         zt = (z + d) % NZ
         in_m.append(rcopy(meta.at[pl.ds(zt, 1)], m1.at[pl.ds(z, 1)], s1m_s.at[d], s1m_r.at[d], dev(zt, y, c, x)))
-    for d in ORDER:
-        zt = (z + d) % NZ
-        yt = (y + d) % NY
-        in_a.append(rcopy(slab.at[zt, :, :, pl.ds(0, HALF)], r1a.at[z], s1a_s.at[d], s1a_r.at[d], dev(zt, y, c, x)))
-        in_b.append(rcopy(slab.at[:, yt, :, pl.ds(HALF, HALF)], r1b.at[y], s1b_s.at[d], s1b_r.at[d], dev(z, yt, c, x)))
+    in_a, in_b = {0: [], 1: []}, {0: [], 1: []}
+    for q in (1, 0):
+        yl, zl = (y + q) % 2, (z + q) % 2
+        for d in ORDER:
+            zt, yt = (z + d) % NZ, (y + d) % NY
+            k = d * 2 + q
+            in_a[q].append(rcopy(
+                slab.at[zt // 2, zt % 2, :, yl, :, pl.ds(0, HALF)], r1a.at[z, yl],
+                s1a_s.at[k], s1a_r.at[k], dev(zt, y, c, x),
+            ))
+            in_b[q].append(rcopy(
+                slab.at[:, zl, yt // 2, yt % 2, :, pl.ds(HALF, HALF)], r1b.at[y, zl],
+                s1b_s.at[k], s1b_r.at[k], dev(z, yt, c, x),
+            ))
 
     for cp in in_m:
         cp.wait_recv()
@@ -104,34 +118,33 @@
             arrive.append(rcopy(m1, m2.at[c, y], s2m_s.at[d * 2 + dc], s2m_r.at[d * 2 + dc], to))
     m2[c, y] = m1[...]
 
-    la.wait()
-    for cp in in_a:
-        cp.wait_recv()
-    for d in ORDER + (0,):
-        for dc in range(2):
-            if d == 0 and dc == 0:
-                continue
-            yt = (y + d) % NY
-            ct = (c + dc) % 2
-            arrive.append(rcopy(
-                r1a.at[:, yt, pl.ds(ct * 4, 4), :], r2a.at[y, :, pl.ds(c * 4, 4), :],
-                s2a_s.at[d * 2 + dc], s2a_r.at[d * 2 + dc], dev(z, yt, ct, x),
-            ))
-    l2a = lcopy(r1a.at[:, y, pl.ds(c * 4, 4), :], r2a.at[y, :, pl.ds(c * 4, 4), :], loc_sem.at[3])
-    lb.wait()
-    for cp in in_b:
-        cp.wait_recv()
-    for d in ORDER + (0,):
-        for dc in range(2):
-            if d == 0 and dc == 0:
-                continue
-            zt = (z + d) % NZ
-            ct = (c + dc) % 2
-            arrive.append(rcopy(
-                r1b.at[:, zt, pl.ds(ct * 4, 4), :], r2b.at[:, z, pl.ds(c * 4, 4), :],
-                s2b_s.at[d * 2 + dc], s2b_r.at[d * 2 + dc], dev(zt, y, ct, x),
-            ))
-    l2b = lcopy(r1b.at[:, z, pl.ds(c * 4, 4), :], r2b.at[:, z, pl.ds(c * 4, 4), :], loc_sem.at[4])
+    for q, order in ((1, (3, 5, 1, 7)), (0, (4, 2, 6, 0))):
+        own[q][0].wait()
+        for cp in in_a[q]:
+            cp.wait_recv()
+        for d in order:
+            for dc in range(2):
+                if d == 0 and dc == 0:
+                    continue
+                yt, ct, k = (y + d) % NY, (c + dc) % 2, d * 2 + dc
+                arrive.append(rcopy(
+                    r1a.at[:, yt % 2, yt // 2, pl.ds(ct * 4, 4), :], r2a.at[y, :, pl.ds(c * 4, 4), :],
+                    s2a_s.at[k], s2a_r.at[k], dev(z, yt, ct, x),
+                ))
+        own[q][1].wait()
+        for cp in in_b[q]:
+            cp.wait_recv()
+        for d in order:
+            for dc in range(2):
+                if d == 0 and dc == 0:
+                    continue
+                zt, ct, k = (z + d) % NZ, (c + dc) % 2, d * 2 + dc
+                arrive.append(rcopy(
+                    r1b.at[:, zt % 2, zt // 2, pl.ds(ct * 4, 4), :], r2b.at[:, z, pl.ds(c * 4, 4), :],
+                    s2b_s.at[k], s2b_r.at[k], dev(zt, y, ct, x),
+                ))
+    l2a = lcopy(r1a.at[:, y % 2, y // 2, pl.ds(c * 4, 4), :], r2a.at[y, :, pl.ds(c * 4, 4), :], loc_sem.at[3])
+    l2b = lcopy(r1b.at[:, z % 2, z // 2, pl.ds(c * 4, 4), :], r2b.at[:, z, pl.ds(c * 4, 4), :], loc_sem.at[4])
 
     n_m = 15
     for cp in arrive[:n_m]:
@@ -167,16 +180,22 @@
     sk[...] = sketch
     save = lcopy(sk, sk_out, loc_sem.at[8])
 
-    def outer(a, b):
-        return lax.dot_general(
-            a, b, (((0,), (0,)), ((), ())), precision=lax.Precision.HIGHEST, preferred_element_type=F32
-        )
-
-    left = sketch[:, :HALF]
-    right = sketch[:, HALF:]
-    gp[pl.ds(0, 128), :] = outer(left, left)
-    gp[pl.ds(128, 128), :] = outer(left, right)
-    gp[pl.ds(256, 128), :] = outer(right, right)
+    turned = jnp.transpose(sketch)
+
+    def pieces(v):
+        first = v.astype(BF16)
+        v = v - first.astype(F32)
+        second = v.astype(BF16)
+        return first, second, (v - second.astype(F32)).astype(BF16)
+
+    ta, tb, tc = pieces(turned)
+    sa, sb, sc = pieces(sketch)
+    gram = jnp.zeros((BPO, BPO), F32)
+    for left, right in ((tc, sa), (ta, sc), (tb, sb), (tb, sa), (ta, sb), (ta, sa)):
+        gram = gram + jnp.dot(left, right, preferred_element_type=F32)
+    gp[pl.ds(0, 128), :] = gram[:HALF, :HALF]
+    gp[pl.ds(128, 128), :] = gram[:HALF, HALF:]
+    gp[pl.ds(256, 128), :] = gram[HALF:, HALF:]
 
     e = x * 2 + c
     near = [(d, dc) for d in (2, 1, 3, 0) for dc in range(2) if d or dc]
@@ -240,34 +259,36 @@
 
 def recip(v):
     guess = pl.reciprocal(v, approx=True)
-    guess = guess * (2.0 - v * guess)
     return guess * (2.0 - v * guess)
 
 
-def factor_block(groups, k0, emit):
-    n = len(groups)
-    tiles = len(groups[0])
+def factor_block(mats, spread, k0, emit):
+    n = 16
     for p in range(n):
         base = p * 8
-        lead = groups[p]
-        ahead = p + 1 < n
-        column = [splat(lead[0][:, base + j:base + j + 1]) for j in range(8)]
-        d = [[splat(column[j][i:i + 1, :]) for j in range(i + 1)] for i in range(8)]
-        rows = [[splat(t[i:i + 1, :]) for t in lead] for i in range(8)]
-        if ahead:
-            nxt = list(groups[p + 1])
-            side = [splat(nxt[0][:, base + j:base + j + 1]) for j in range(8)]
+        lead = mats[0][base:base + 8, :]
+        at = (p % 2) * 64
+        for j in range(8):
+            spread[at + j * 8:at + j * 8 + 8, :] = splat(lead[:, base + j:base + j + 1])
+        d = [[spread[pl.ds(at + j * 8 + i, 8, stride=0), :] for j in range(i + 1)] for i in range(8)]
+        rows = [[m[pl.ds(base + i, 8, stride=0), :] for m in mats] for i in range(8)]
+        near = list(range(p + 1, min(p + 3, n)))
+        blocks = {g: [m[g * 8:g * 8 + 8, :] for m in mats] for g in near}
+        side = {g: [splat(blocks[g][0][:, base + j:base + j + 1]) for j in range(8)] for g in near}
         final = []
         for b in range(0, 8, 2):
             p00, p10, p11 = d[b][b], d[b + 1][b], d[b + 1][b + 1]
             inv = recip(p00 * p11 - p10 * p10)
             x0, x1 = rows[b], rows[b + 1]
-            if ahead:
-                m0 = (p11 * side[b] - p10 * side[b + 1]) * inv
-                m1 = (p00 * side[b + 1] - p10 * side[b]) * inv
-                nxt = [t - (m0 * x0[k] + m1 * x1[k]) for k, t in enumerate(nxt)]
+            for g in near:
+                v = side[g]
+                n0 = p11 * v[b] - p10 * v[b + 1]
+                n1 = p00 * v[b + 1] - p10 * v[b]
+                blocks[g] = [t - (n0 * x0[k] + n1 * x1[k]) * inv for k, t in enumerate(blocks[g])]
+                if b < 6:
+                    n0, n1 = n0 * inv, n1 * inv
                 for i in range(b + 2, 8):
-                    side[i] = side[i] - (m0 * d[i][b] + m1 * d[i][b + 1])
+                    v[i] = v[i] - (n0 * d[i][b] + n1 * d[i][b + 1])
             for i in range(b + 2, 8):
                 n0 = p11 * d[i][b] - p10 * d[i][b + 1]
                 n1 = p00 * d[i][b + 1] - p10 * d[i][b]
@@ -281,23 +302,25 @@
             first = [t * r0 for t in x0]
             final.append(first)
             final.append([(t - low * first[k]) * r1 for k, t in enumerate(x1)])
+        for g in near:
+            for k, m in enumerate(mats):
+                m[g * 8:g * 8 + 8, :] = blocks[g][k]
         for j in range(8):
             emit(k0 + base + j, base + j, [t[0:1, :] for t in final[j]])
-        if ahead:
-            groups[p + 1] = nxt
-        if p + 2 < n:
-            panel = jnp.concatenate([final[j][0][0:1, :] for j in range(8)], axis=0)
-            turned = jnp.transpose(panel)
-            for g in range(p + 2, n):
-                mult = [splat(turned[g * 8:g * 8 + 8, j:j + 1]) for j in range(8)]
-                for k in range(tiles):
-                    terms = [mult[j] * final[j][k] for j in range(8)]
-                    while len(terms) > 1:
-                        terms = [terms[i] + terms[i + 1] for i in range(0, len(terms), 2)]
-                    groups[g][k] = groups[g][k] - terms[0]
-
-
-def factor_kernel(scale, g_ref, sk_ref, f_out, sk_out, sem):
+        if p + 3 < n:
+            first = (p + 3) * 8
+            panel = [
+                jnp.concatenate([final[j][k][0:1, :] for j in range(8)], axis=0) for k in range(len(mats))
+            ]
+            for k, m in enumerate(mats):
+                less = lax.dot_general(
+                    panel[0], panel[k], (((0,), (0,)), ((), ())),
+                    precision=lax.Precision.HIGHEST, preferred_element_type=F32,
+                )
+                m[first:, :] = m[first:, :] - less[first:, :]
+
+
+def factor_kernel(scale, g_ref, sk_ref, f_out, sk_out, a0, a1, spread, sem):
     cp = pltpu.make_async_copy(sk_ref, sk_out, sem)
     cp.start()
     lane = lax.broadcasted_iota(jnp.int32, (8, HALF), 1)
@@ -319,29 +342,23 @@
                 if k == 0:
                     v = jnp.where(lane[0:1, :] >= diagonal, v, 0.0)
                 f_out[at:at + 1, (first + k) * HALF:(first + k + 1) * HALF] = v
-                if keep is not None and k == 1:
-                    keep.append(values[1])
         return put
 
-    keep = []
-    top = []
     for p in range(16):
-        top.append([
-            g_ref[p * 8:p * 8 + 8, :] * (down[0][p] * scaled[0]),
-            g_ref[128 + p * 8:128 + p * 8 + 8, :] * (down[0][p] * scaled[1]),
-        ])
+        at = p * 8
+        a0[at:at + 8, :] = g_ref[at:at + 8, :] * (down[0][p] * scaled[0])
+        a1[at:at + 8, :] = g_ref[128 + at:128 + at + 8, :] * (down[0][p] * scaled[1])
     f_out[128:256, 0:128] = jnp.zeros((128, 128), F32)
-    factor_block(top, 0, emit(0))
-    corner = jnp.concatenate(keep, axis=0)
-    keep = None
+    factor_block([a0, a1], spread, 0, emit(0))
+    corner = f_out[0:128, 128:256]
     less = lax.dot_general(
         corner, corner, (((0,), (0,)), ((), ())), precision=lax.Precision.HIGHEST, preferred_element_type=F32
     )
-    bottom = []
     for p in range(16):
-        at = 256 + p * 8
-        bottom.append([g_ref[at:at + 8, :] * (down[1][p] * scaled[1]) - less[p * 8:p * 8 + 8, :]])
-    factor_block(bottom, 128, emit(1))
+        at = p * 8
+        left = g_ref[256 + at:256 + at + 8, :] - less[at:at + 8, :] * (1.0 / scale)
+        a0[at:at + 8, :] = left * (down[1][p] * scaled[1])
+    factor_block([a0], spread, 128, emit(1))
     cp.wait()
 
 
@@ -358,14 +375,14 @@
         in_specs=[hbm] * 4,
         out_specs=(hbm, vm),
         scratch_shapes=[
-            pltpu.VMEM((8, 8, 8, 256), F32),
+            pltpu.VMEM((4, 2, 4, 2, 8, 256), F32),
             pltpu.VMEM((1, 512), jnp.int32),
             pltpu.VMEM((1, 512), jnp.int32),
             pltpu.VMEM((1, 128), jnp.int32),
             pltpu.VMEM((256, 256), F32),
             pltpu.VMEM((8, 128), jnp.int32),
-            pltpu.VMEM((8, 8, 8, 128), F32),
-            pltpu.VMEM((8, 8, 8, 128), F32),
+            pltpu.VMEM((8, 2, 4, 8, 128), F32),
+            pltpu.VMEM((8, 2, 4, 8, 128), F32),
             pltpu.VMEM((8, 8, 8, 128), F32),
             pltpu.VMEM((8, 8, 8, 128), F32),
             pltpu.VMEM((8, 128), jnp.int32),
@@ -379,8 +396,8 @@
             pltpu.VMEM((8, 8, 128), F32),
             pltpu.VMEM((48, 128), F32),
             pltpu.VMEM((384, 128), F32),
-            dma((9,)),
-            dma((8,)), dma((8,)), dma((8,)), dma((8,)), dma((8,)), dma((8,)),
+            dma((13,)),
+            dma((16,)), dma((16,)), dma((16,)), dma((16,)), dma((8,)), dma((8,)),
             dma((16,)), dma((16,)), dma((16,)), dma((16,)), dma((16,)), dma((16,)),
             dma((8,)), dma((8,)), dma((8,)), dma((8,)), dma((8,)), dma((8,)),
             dma((8,)), dma((8,)), dma((8,)), dma((8,)),
@@ -388,14 +405,19 @@
         compiler_params=pltpu.CompilerParams(
             collective_id=0, has_side_effects=True, vmem_limit_bytes=60 * 1024 * 1024
         ),
-    )(slab.reshape(8, 8, 8, width), buckets, signs, counts)
+    )(slab.reshape(4, 2, 4, 2, 8, width), buckets, signs, counts)
     slots = float(lax.axis_size("grp") * owners * owners * capacity)
     factor, sketch = pl.pallas_call(
         lambda *refs: factor_kernel(1.0 / slots, *refs),
         out_shape=(jax.ShapeDtypeStruct((width, width), F32), jax.ShapeDtypeStruct((BPO, width), F32)),
         in_specs=[vm, hbm],
         out_specs=(vm, hbm),
-        scratch_shapes=[pltpu.SemaphoreType.DMA],
+        scratch_shapes=[
+            pltpu.VMEM((HALF, HALF), F32),
+            pltpu.VMEM((HALF, HALF), F32),
+            pltpu.VMEM((HALF, HALF), F32),
+            pltpu.SemaphoreType.DMA,
+        ],
         compiler_params=pltpu.CompilerParams(vmem_limit_bytes=60 * 1024 * 1024),
     )(gram, sketch)
     return (sketch.reshape(1, BPO, width), factor)

time: 70.4 us -> 68.5 us (0.973)
  Pallas kernels: 69.6 us -> 67.7 us
    pallas_call x1, Pallas kernels: 12 us -> 10.7 us  [body(): pl.pallas_call(lambda *refs: factor_kernel(1.0 / slots, *refs), out_shape...]
where the time goes in v4:
time: 68.5 us; the launch traced here: 68.3 us
  Pallas kernels  67.7 us (99%)
    pallas_call x1, Pallas kernels, body(): pl.pallas_call(gram_kernel, out_shape=(jax.ShapeDtypeStruct((BPO, width),...  57 us
    pallas_call x1, Pallas kernels, body(): pl.pallas_call(lambda *refs: factor_kernel(1.0 / slots, *refs), out_shape...  10.7 us

profile of v4, /device:TPU:1, one launch (start us, length us, event | category | flops | bytes accessed | tf_op | source)
XLA Modules:
  0.0 68.3 jit_solution(15773577566003948327)
XLA Ops:
  0.6 57.0 %shard_map.59 = (f32[256,256]{1,0:T(8,128)}, f32[384,128]{1,0:T(8,128)}) custom-call(f32[4,2,4,2,8,256]{5,4,3,2,1,0:T(8,128)} %bitcast.2, s32[1,512]{1,0:T(1,128)} %buckets_hbm.1, s32[1,512]{1,0:T(1,128)} %signs_hbm.1, s32[1,128]{1,0:T(1,128)} %counts_hbm.1), custom_call_target="tpu_custom_call" | custom-call | tf_op jit(solution)/shard_map/pallas_call | solution.py:372
  57.7 10.7 %shard_map.60 = (f32[256,256]{1,0:T(8,128)}, f32[256,256]{1,0:T(8,128)}) custom-call(f32[384,128]{1,0:T(8,128)} %get-tuple-element.6.refs_0_, f32[256,256]{1,0:T(8,128)} %get-tuple-element.7.refs_1_), custom_call_target="tpu_custom_call" | custom-call | tf_op jit(solution)/shard_map/pallas_call | solution.py:410

commit v5 on v4

--- a/solution.py
+++ b/solution.py
@@ -17,8 +17,8 @@
 
 
 def gram_kernel(
-    slab_hbm, buckets_hbm, signs_hbm, counts_hbm, sk_out, g_out,
-    slab, buckets, signs, counts, sk, meta, r1a, r1b, r2a, r2b, m1, m2, mt, gp, gx, acc, gz, part, gy, fin, gfull,
+    slab, buckets_hbm, signs_hbm, counts_hbm, sk_out, g_out,
+    buckets, signs, counts, sk, meta, r1a, r1b, r2a, r2b, m1, m2, mt, gp, gx, acc, gz, part, gy, fin, gfull,
     loc_sem, s1a_s, s1a_r, s1b_s, s1b_r, s1m_s, s1m_r, s2a_s, s2a_r, s2b_s, s2b_r, s2m_s, s2m_r,
     x_s, x_r, z_s, z_r, y_s, y_r, zg_s, zg_r, xg_s, xg_r,
 ):
@@ -40,6 +40,17 @@
     for d in range(1, 4):
         for dc in range(2):
             peers.append(dev(z, y, (c + dc) % 2, (x + d) % NX))
+
+    def lcopy(src, dst, sem):
+        cp = pltpu.make_async_copy(src, dst, sem)
+        cp.start()
+        return cp
+
+    small = [
+        lcopy(counts_hbm, counts, loc_sem.at[5]),
+        lcopy(signs_hbm, signs, loc_sem.at[6]),
+        lcopy(buckets_hbm, buckets, loc_sem.at[7]),
+    ]
     for p in peers:
         pl.semaphore_signal(barrier, inc=1, device_id=p, device_id_type=MESH)
 
@@ -53,17 +64,32 @@
         sends.append(cp)
         return cp
 
-    def lcopy(src, dst, sem):
-        cp = pltpu.make_async_copy(src, dst, sem)
-        cp.start()
-        return cp
-
-    load = lcopy(slab_hbm, slab, loc_sem.at[2])
-    small = [
-        lcopy(counts_hbm, counts, loc_sem.at[5]),
-        lcopy(signs_hbm, signs, loc_sem.at[6]),
-        lcopy(buckets_hbm, buckets, loc_sem.at[7]),
-    ]
+    own = {}
+    for q in range(2):
+        yl, zl = (y + q) % 2, (z + q) % 2
+        own[q] = (
+            lcopy(slab.at[z // 2, z % 2, :, yl, :, pl.ds(0, HALF)], r1a.at[z, yl], loc_sem.at[9 + q]),
+            lcopy(slab.at[:, zl, y // 2, y % 2, :, pl.ds(HALF, HALF)], r1b.at[y, zl], loc_sem.at[11 + q]),
+        )
+    pl.semaphore_wait(barrier, len(peers))
+
+    in_a, in_b = {0: [], 1: []}, {0: [], 1: []}
+
+    def first_stage(q):
+        yl, zl = (y + q) % 2, (z + q) % 2
+        for d in ORDER:
+            zt, yt = (z + d) % NZ, (y + d) % NY
+            k = d * 2 + q
+            in_a[q].append(rcopy(
+                slab.at[zt // 2, zt % 2, :, yl, :, pl.ds(0, HALF)], r1a.at[z, yl],
+                s1a_s.at[k], s1a_r.at[k], dev(zt, y, c, x),
+            ))
+            in_b[q].append(rcopy(
+                slab.at[:, zl, yt // 2, yt % 2, :, pl.ds(HALF, HALF)], r1b.at[y, zl],
+                s1b_s.at[k], s1b_r.at[k], dev(z, yt, c, x),
+            ))
+
+    first_stage(1)
     slot = lax.broadcasted_iota(jnp.int32, (HALF, 512), 1)
     pair = lax.broadcasted_iota(jnp.int32, (HALF, 512), 0)
     spread = jnp.where(slot // 4 == pair, 1.0, 0.0).astype(BF16)
@@ -77,48 +103,15 @@
     for t in range(NZ):
         meta[t:t + 1, 0:64] = buckets[0:1, t * 64:t * 64 + 64]
         meta[t:t + 1, 64:128] = weight[0:1, t * 64:t * 64 + 64]
-    load.wait()
-    own = {}
-    for q in range(2):
-        yl, zl = (y + q) % 2, (z + q) % 2
-        own[q] = (
-            lcopy(slab.at[z // 2, z % 2, :, yl, :, pl.ds(0, HALF)], r1a.at[z, yl], loc_sem.at[9 + q]),
-            lcopy(slab.at[:, zl, y // 2, y % 2, :, pl.ds(HALF, HALF)], r1b.at[y, zl], loc_sem.at[11 + q]),
-        )
     m1[pl.ds(z, 1), :] = meta[pl.ds(z, 1), :]
-    pl.semaphore_wait(barrier, len(peers))
-
     in_m = []
     for d in ORDER:
         zt = (z + d) % NZ
         in_m.append(rcopy(meta.at[pl.ds(zt, 1)], m1.at[pl.ds(z, 1)], s1m_s.at[d], s1m_r.at[d], dev(zt, y, c, x)))
-    in_a, in_b = {0: [], 1: []}, {0: [], 1: []}
-    for q in (1, 0):
-        yl, zl = (y + q) % 2, (z + q) % 2
-        for d in ORDER:
-            zt, yt = (z + d) % NZ, (y + d) % NY
-            k = d * 2 + q
-            in_a[q].append(rcopy(
-                slab.at[zt // 2, zt % 2, :, yl, :, pl.ds(0, HALF)], r1a.at[z, yl],
-                s1a_s.at[k], s1a_r.at[k], dev(zt, y, c, x),
-            ))
-            in_b[q].append(rcopy(
-                slab.at[:, zl, yt // 2, yt % 2, :, pl.ds(HALF, HALF)], r1b.at[y, zl],
-                s1b_s.at[k], s1b_r.at[k], dev(z, yt, c, x),
-            ))
-
-    for cp in in_m:
-        cp.wait_recv()
-    arrive = []
-    for d in ORDER + (0,):
-        for dc in range(2):
-            if d == 0 and dc == 0:
-                continue
-            to = dev(z, (y + d) % NY, (c + dc) % 2, x)
-            arrive.append(rcopy(m1, m2.at[c, y], s2m_s.at[d * 2 + dc], s2m_r.at[d * 2 + dc], to))
-    m2[c, y] = m1[...]
-
-    for q, order in ((1, (3, 5, 1, 7)), (0, (4, 2, 6, 0))):
+    first_stage(0)
+    arrive, arrive_m = [], []
+
+    def second_stage(q, order):
         own[q][0].wait()
         for cp in in_a[q]:
             cp.wait_recv()
@@ -143,11 +136,21 @@
                     r1b.at[:, zt % 2, zt // 2, pl.ds(ct * 4, 4), :], r2b.at[:, z, pl.ds(c * 4, 4), :],
                     s2b_s.at[k], s2b_r.at[k], dev(zt, y, ct, x),
                 ))
+    second_stage(1, (3, 5, 1, 7))
+    for cp in in_m:
+        cp.wait_recv()
+    for d in ORDER + (0,):
+        for dc in range(2):
+            if d == 0 and dc == 0:
+                continue
+            to = dev(z, (y + d) % NY, (c + dc) % 2, x)
+            arrive_m.append(rcopy(m1, m2.at[c, y], s2m_s.at[d * 2 + dc], s2m_r.at[d * 2 + dc], to))
+    m2[c, y] = m1[...]
+    second_stage(0, (4, 2, 6, 0))
     l2a = lcopy(r1a.at[:, y % 2, y // 2, pl.ds(c * 4, 4), :], r2a.at[y, :, pl.ds(c * 4, 4), :], loc_sem.at[3])
     l2b = lcopy(r1b.at[:, z % 2, z // 2, pl.ds(c * 4, 4), :], r2b.at[:, z, pl.ds(c * 4, 4), :], loc_sem.at[4])
 
-    n_m = 15
-    for cp in arrive[:n_m]:
+    for cp in arrive_m:
         cp.wait_recv()
     mt[...] = jnp.transpose(m2[...].reshape(128, 128))
     b4 = mt[pl.ds(y * 8 + c * 4, 4), :]
@@ -157,7 +160,7 @@
         [jnp.where(row == b4[s:s + 1, :], w4[s:s + 1, :], 0).astype(F32) for s in range(4)], axis=1
     ).astype(BF16)
 
-    for cp in arrive[n_m:]:
+    for cp in arrive:
         cp.wait_recv()
     l2a.wait()
     l2b.wait()
@@ -262,19 +265,22 @@
     return guess * (2.0 - v * guess)
 
 
-def factor_block(mats, spread, k0, emit):
+def factor_block(mats, spread, turn, k0, emit):
     n = 16
     for p in range(n):
         base = p * 8
-        lead = mats[0][base:base + 8, :]
         at = (p % 2) * 64
+        if p == 0:
+            ahead = [splat(mats[0][0:8, :][:, j:j + 1]) for j in range(8)]
         for j in range(8):
-            spread[at + j * 8:at + j * 8 + 8, :] = splat(lead[:, base + j:base + j + 1])
+            spread[at + j * 8:at + j * 8 + 8, :] = ahead[j]
         d = [[spread[pl.ds(at + j * 8 + i, 8, stride=0), :] for j in range(i + 1)] for i in range(8)]
         rows = [[m[pl.ds(base + i, 8, stride=0), :] for m in mats] for i in range(8)]
         near = list(range(p + 1, min(p + 3, n)))
         blocks = {g: [m[g * 8:g * 8 + 8, :] for m in mats] for g in near}
         side = {g: [splat(blocks[g][0][:, base + j:base + j + 1]) for j in range(8)] for g in near}
+        if near:
+            ahead = [splat(blocks[p + 1][0][:, base + 8 + j:base + 9 + j]) for j in range(8)]
         final = []
         for b in range(0, 8, 2):
             p00, p10, p11 = d[b][b], d[b + 1][b], d[b + 1][b + 1]
@@ -285,6 +291,14 @@
                 n0 = p11 * v[b] - p10 * v[b + 1]
                 n1 = p00 * v[b + 1] - p10 * v[b]
                 blocks[g] = [t - (n0 * x0[k] + n1 * x1[k]) * inv for k, t in enumerate(blocks[g])]
+                if g == p + 1:
+                    to = at + b * 8
+                    turn[to:to + 8, :] = v[b]
+                    turn[to + 8:to + 16, :] = v[b + 1]
+                    for j in range(8):
+                        s0 = turn[pl.ds(to + j, 8, stride=0), :]
+                        s1 = turn[pl.ds(to + 8 + j, 8, stride=0), :]
+                        ahead[j] = ahead[j] - (n0 * s0 + n1 * s1) * inv
                 if b < 6:
                     n0, n1 = n0 * inv, n1 * inv
                 for i in range(b + 2, 8):
@@ -320,7 +334,7 @@
                 m[first:, :] = m[first:, :] - less[first:, :]
 
 
-def factor_kernel(scale, g_ref, sk_ref, f_out, sk_out, a0, a1, spread, sem):
+def factor_kernel(scale, g_ref, sk_ref, f_out, sk_out, a0, a1, spread, turn, sem):
     cp = pltpu.make_async_copy(sk_ref, sk_out, sem)
     cp.start()
     lane = lax.broadcasted_iota(jnp.int32, (8, HALF), 1)
@@ -349,7 +363,7 @@
         a0[at:at + 8, :] = g_ref[at:at + 8, :] * (down[0][p] * scaled[0])
         a1[at:at + 8, :] = g_ref[128 + at:128 + at + 8, :] * (down[0][p] * scaled[1])
     f_out[128:256, 0:128] = jnp.zeros((128, 128), F32)
-    factor_block([a0, a1], spread, 0, emit(0))
+    factor_block([a0, a1], spread, turn, 0, emit(0))
     corner = f_out[0:128, 128:256]
     less = lax.dot_general(
         corner, corner, (((0,), (0,)), ((), ())), precision=lax.Precision.HIGHEST, preferred_element_type=F32
@@ -358,7 +372,7 @@
         at = p * 8
         left = g_ref[256 + at:256 + at + 8, :] - less[at:at + 8, :] * (1.0 / scale)
         a0[at:at + 8, :] = left * (down[1][p] * scaled[1])
-    factor_block([a0], spread, 128, emit(1))
+    factor_block([a0], spread, turn, 128, emit(1))
     cp.wait()
 
 
@@ -375,7 +389,6 @@
         in_specs=[hbm] * 4,
         out_specs=(hbm, vm),
         scratch_shapes=[
-            pltpu.VMEM((4, 2, 4, 2, 8, 256), F32),
             pltpu.VMEM((1, 512), jnp.int32),
             pltpu.VMEM((1, 512), jnp.int32),
             pltpu.VMEM((1, 128), jnp.int32),
@@ -416,6 +429,7 @@
             pltpu.VMEM((HALF, HALF), F32),
             pltpu.VMEM((HALF, HALF), F32),
             pltpu.VMEM((HALF, HALF), F32),
+            pltpu.VMEM((HALF, HALF), F32),
             pltpu.SemaphoreType.DMA,
         ],
         compiler_params=pltpu.CompilerParams(vmem_limit_bytes=60 * 1024 * 1024),

time: 68.5 us -> 69.6 us (1.016)
  Pallas kernels: 67.7 us -> 68.8 us
    pallas_call x1, Pallas kernels: 57 us -> 58.1 us  [body(): pl.pallas_call(gram_kernel, out_shape=(jax.ShapeDtypeStruct((BPO, width),...]
where the time goes in v5:
time: 69.6 us; the launch traced here: 69.4 us
  Pallas kernels  68.8 us (99%)
    pallas_call x1, Pallas kernels, body(): pl.pallas_call(gram_kernel, out_shape=(jax.ShapeDtypeStruct((BPO, width),...  58.1 us
    pallas_call x1, Pallas kernels, body(): pl.pallas_call(lambda *refs: factor_kernel(1.0 / slots, *refs), out_shape...  10.7 us

profile of v5, /device:TPU:1, one launch (start us, length us, event | category | flops | bytes accessed | tf_op | source)
XLA Modules:
  0.0 69.4 jit_solution(17230684143446428360)
XLA Ops:
  0.6 58.1 %shard_map.59 = (f32[256,256]{1,0:T(8,128)}, f32[384,128]{1,0:T(8,128)}) custom-call(f32[4,2,4,2,8,256]{5,4,3,2,1,0:T(8,128)} %bitcast.2, s32[1,512]{1,0:T(1,128)} %buckets_hbm.1, s32[1,512]{1,0:T(1,128)} %signs_hbm.1, s32[1,128]{1,0:T(1,128)} %counts_hbm.1), custom_call_target="tpu_custom_call" | custom-call | tf_op jit(solution)/shard_map/pallas_call | solution.py:386
  58.7 10.7 %shard_map.60 = (f32[256,256]{1,0:T(8,128)}, f32[256,256]{1,0:T(8,128)}) custom-call(f32[384,128]{1,0:T(8,128)} %get-tuple-element.6.refs_0_, f32[256,256]{1,0:T(8,128)} %get-tuple-element.7.refs_1_), custom_call_target="tpu_custom_call" | custom-call | tf_op jit(solution)/shard_map/pallas_call | solution.py:423

commit v6 on v4

--- a/solution.py
+++ b/solution.py
@@ -262,29 +262,50 @@
     return guess * (2.0 - v * guess)
 
 
-def factor_block(mats, spread, k0, emit):
-    n = 16
-    for p in range(n):
-        base = p * 8
-        lead = mats[0][base:base + 8, :]
-        at = (p % 2) * 64
-        for j in range(8):
-            spread[at + j * 8:at + j * 8 + 8, :] = splat(lead[:, base + j:base + j + 1])
-        d = [[spread[pl.ds(at + j * 8 + i, 8, stride=0), :] for j in range(i + 1)] for i in range(8)]
+def factor_block(mats, spread, turn, panels, put):
+    for j in range(8):
+        spread[j * 8:j * 8 + 8, :] = splat(mats[0][0:8, :][:, j:j + 1])
+    for k in range(len(mats)):
+        panels[k * 8:k * 8 + 8, :] = jnp.zeros((8, HALF), F32)
+    index = lax.broadcasted_iota(jnp.int32, (HALF, HALF), 0)
+
+    def step(p, carry):
+        base = pl.multiple_of(p * 8, 8)
+        back_by = lax.rem(HALF - base, HALF)
+        d = [[spread[pl.ds(j * 8 + i, 8, stride=0), :] for j in range(i + 1)] for i in range(8)]
         rows = [[m[pl.ds(base + i, 8, stride=0), :] for m in mats] for i in range(8)]
-        near = list(range(p + 1, min(p + 3, n)))
-        blocks = {g: [m[g * 8:g * 8 + 8, :] for m in mats] for g in near}
-        side = {g: [splat(blocks[g][0][:, base + j:base + j + 1]) for j in range(8)] for g in near}
+        blocks = {1: [m[pl.ds(base + 8, 8), :] for m in mats]}
+        rolled = pltpu.roll(blocks[1][0], back_by, 1)
+        side = {1: [splat(rolled[:, j:j + 1]) for j in range(8)]}
+        ahead = [splat(rolled[:, 8 + j:9 + j]) for j in range(8)]
+        before = [panels[k * 8:k * 8 + 8, :] for k in range(len(mats))]
+        for k, m in enumerate(mats):
+            less = lax.dot_general(
+                before[0], before[k], (((0,), (0,)), ((), ())),
+                precision=lax.Precision.HIGHEST, preferred_element_type=F32,
+            )
+            m[0:HALF, :] = m[0:HALF, :] - jnp.where(index >= base + 16, less, 0.0)
+        blocks[2] = [m[pl.ds(base + 16, 8), :] for m in mats]
+        rolled = pltpu.roll(blocks[2][0], back_by, 1)
+        side[2] = [splat(rolled[:, j:j + 1]) for j in range(8)]
         final = []
         for b in range(0, 8, 2):
             p00, p10, p11 = d[b][b], d[b + 1][b], d[b + 1][b + 1]
             inv = recip(p00 * p11 - p10 * p10)
             x0, x1 = rows[b], rows[b + 1]
-            for g in near:
+            for g in (1, 2):
                 v = side[g]
                 n0 = p11 * v[b] - p10 * v[b + 1]
                 n1 = p00 * v[b + 1] - p10 * v[b]
                 blocks[g] = [t - (n0 * x0[k] + n1 * x1[k]) * inv for k, t in enumerate(blocks[g])]
+                if g == 1:
+                    to = b * 8
+                    turn[to:to + 8, :] = v[b]
+                    turn[to + 8:to + 16, :] = v[b + 1]
+                    for j in range(8):
+                        s0 = turn[pl.ds(to + j, 8, stride=0), :]
+                        s1 = turn[pl.ds(to + 8 + j, 8, stride=0), :]
+                        ahead[j] = ahead[j] - (n0 * s0 + n1 * s1) * inv
                 if b < 6:
                     n0, n1 = n0 * inv, n1 * inv
                 for i in range(b + 2, 8):
@@ -302,25 +323,20 @@
             first = [t * r0 for t in x0]
             final.append(first)
             final.append([(t - low * first[k]) * r1 for k, t in enumerate(x1)])
-        for g in near:
-            for k, m in enumerate(mats):
-                m[g * 8:g * 8 + 8, :] = blocks[g][k]
         for j in range(8):
-            emit(k0 + base + j, base + j, [t[0:1, :] for t in final[j]])
-        if p + 3 < n:
-            first = (p + 3) * 8
-            panel = [
-                jnp.concatenate([final[j][k][0:1, :] for j in range(8)], axis=0) for k in range(len(mats))
-            ]
-            for k, m in enumerate(mats):
-                less = lax.dot_general(
-                    panel[0], panel[k], (((0,), (0,)), ((), ())),
-                    precision=lax.Precision.HIGHEST, preferred_element_type=F32,
-                )
-                m[first:, :] = m[first:, :] - less[first:, :]
-
-
-def factor_kernel(scale, g_ref, sk_ref, f_out, sk_out, a0, a1, spread, sem):
+            spread[j * 8:j * 8 + 8, :] = ahead[j]
+        for k, m in enumerate(mats):
+            m[pl.ds(base + 8, 8), :] = blocks[1][k]
+            m[pl.ds(base + 16, 8), :] = blocks[2][k]
+            panel = jnp.concatenate([final[j][k][0:1, :] for j in range(8)], axis=0)
+            panels[k * 8:k * 8 + 8, :] = panel
+            put(base, k, panel)
+        return carry
+
+    lax.fori_loop(0, 16, step, 0)
+
+
+def factor_kernel(scale, g_ref, sk_ref, f_out, sk_out, a0, a1, spread, turn, panels, sem):
     cp = pltpu.make_async_copy(sk_ref, sk_out, sem)
     cp.start()
     lane = lax.broadcasted_iota(jnp.int32, (8, HALF), 1)
@@ -335,21 +351,23 @@
     scaled = [lax.rsqrt(v) for v in across]
     back = [jnp.sqrt(v * scale) for v in across]
 
-    def emit(first):
-        def put(at, diagonal, values):
-            for k, v in enumerate(values):
-                v = v * back[first + k][0:1, :]
-                if k == 0:
-                    v = jnp.where(lane[0:1, :] >= diagonal, v, 0.0)
-                f_out[at:at + 1, (first + k) * HALF:(first + k + 1) * HALF] = v
+    def put_at(first):
+        def put(base, k, panel):
+            panel = panel * back[first + k]
+            if k == 0:
+                panel = jnp.where(lane >= sub + base, panel, 0.0)
+            lanes = slice((first + k) * HALF, (first + k + 1) * HALF)
+            f_out[pl.ds(first * HALF + base, 8), lanes] = panel
         return put
 
+    a0[HALF:HALF + 16, :] = jnp.zeros((16, HALF), F32)
+    a1[HALF:HALF + 16, :] = jnp.zeros((16, HALF), F32)
     for p in range(16):
         at = p * 8
         a0[at:at + 8, :] = g_ref[at:at + 8, :] * (down[0][p] * scaled[0])
         a1[at:at + 8, :] = g_ref[128 + at:128 + at + 8, :] * (down[0][p] * scaled[1])
     f_out[128:256, 0:128] = jnp.zeros((128, 128), F32)
-    factor_block([a0, a1], spread, 0, emit(0))
+    factor_block([a0, a1], spread, turn, panels, put_at(0))
     corner = f_out[0:128, 128:256]
     less = lax.dot_general(
         corner, corner, (((0,), (0,)), ((), ())), precision=lax.Precision.HIGHEST, preferred_element_type=F32
@@ -358,7 +376,7 @@
         at = p * 8
         left = g_ref[256 + at:256 + at + 8, :] - less[at:at + 8, :] * (1.0 / scale)
         a0[at:at + 8, :] = left * (down[1][p] * scaled[1])
-    factor_block([a0], spread, 128, emit(1))
+    factor_block([a0], spread, turn, panels, put_at(1))
     cp.wait()
 
 
@@ -413,9 +431,11 @@
         in_specs=[vm, hbm],
         out_specs=(vm, hbm),
         scratch_shapes=[
-            pltpu.VMEM((HALF, HALF), F32),
-            pltpu.VMEM((HALF, HALF), F32),
-            pltpu.VMEM((HALF, HALF), F32),
+            pltpu.VMEM((HALF + 16, HALF), F32),
+            pltpu.VMEM((HALF + 16, HALF), F32),
+            pltpu.VMEM((64, HALF), F32),
+            pltpu.VMEM((64, HALF), F32),
+            pltpu.VMEM((16, HALF), F32),
             pltpu.SemaphoreType.DMA,
         ],
         compiler_params=pltpu.CompilerParams(vmem_limit_bytes=60 * 1024 * 1024),

time: 68.5 us -> 75 us (1.095)
  Pallas kernels: 67.7 us -> 74.2 us
    pallas_call x1, Pallas kernels: 10.7 us -> 17.2 us  [body(): pl.pallas_call(lambda *refs: factor_kernel(1.0 / slots, *refs), out_shape...]
where the time goes in v6:
time: 75 us; the launch traced here: 74.8 us
  Pallas kernels  74.2 us (99%)
    pallas_call x1, Pallas kernels, body(): pl.pallas_call(gram_kernel, out_shape=(jax.ShapeDtypeStruct((BPO, width),...  57 us
    pallas_call x1, Pallas kernels, body(): pl.pallas_call(lambda *refs: factor_kernel(1.0 / slots, *refs), out_shape...  17.2 us

profile of v6, /device:TPU:1, one launch (start us, length us, event | category | flops | bytes accessed | tf_op | source)
XLA Modules:
  0.0 74.8 jit_solution(7421914147770003436)
XLA Ops:
  0.6 57.0 %shard_map.59 = (f32[256,256]{1,0:T(8,128)}, f32[384,128]{1,0:T(8,128)}) custom-call(f32[4,2,4,2,8,256]{5,4,3,2,1,0:T(8,128)} %bitcast.2, s32[1,512]{1,0:T(1,128)} %buckets_hbm.1, s32[1,512]{1,0:T(1,128)} %signs_hbm.1, s32[1,128]{1,0:T(1,128)} %counts_hbm.1), custom_call_target="tpu_custom_call" | custom-call | tf_op jit(solution)/shard_map/pallas_call | solution.py:390
  57.7 17.2 %shard_map.60 = (f32[256,256]{1,0:T(8,128)}, f32[256,256]{1,0:T(8,128)}) custom-call(f32[384,128]{1,0:T(8,128)} %get-tuple-element.6.refs_0_, f32[256,256]{1,0:T(8,128)} %get-tuple-element.7.refs_1_), custom_call_target="tpu_custom_call" | custom-call | tf_op jit(solution)/shard_map/pallas_call | solution.py:428

commit v7 on v4

--- a/solution.py
+++ b/solution.py
@@ -262,19 +262,22 @@
     return guess * (2.0 - v * guess)
 
 
-def factor_block(mats, spread, k0, emit):
+def factor_block(mats, spread, turn, k0, emit):
     n = 16
     for p in range(n):
         base = p * 8
-        lead = mats[0][base:base + 8, :]
         at = (p % 2) * 64
+        if p == 0:
+            ahead = [splat(mats[0][0:8, :][:, j:j + 1]) for j in range(8)]
         for j in range(8):
-            spread[at + j * 8:at + j * 8 + 8, :] = splat(lead[:, base + j:base + j + 1])
+            spread[at + j * 8:at + j * 8 + 8, :] = ahead[j]
         d = [[spread[pl.ds(at + j * 8 + i, 8, stride=0), :] for j in range(i + 1)] for i in range(8)]
         rows = [[m[pl.ds(base + i, 8, stride=0), :] for m in mats] for i in range(8)]
-        near = list(range(p + 1, min(p + 3, n)))
+        near = list(range(p + 1, min(p + 4, n)))
         blocks = {g: [m[g * 8:g * 8 + 8, :] for m in mats] for g in near}
         side = {g: [splat(blocks[g][0][:, base + j:base + j + 1]) for j in range(8)] for g in near}
+        if near:
+            ahead = [splat(blocks[p + 1][0][:, base + 8 + j:base + 9 + j]) for j in range(8)]
         final = []
         for b in range(0, 8, 2):
             p00, p10, p11 = d[b][b], d[b + 1][b], d[b + 1][b + 1]
@@ -285,6 +288,14 @@
                 n0 = p11 * v[b] - p10 * v[b + 1]
                 n1 = p00 * v[b + 1] - p10 * v[b]
                 blocks[g] = [t - (n0 * x0[k] + n1 * x1[k]) * inv for k, t in enumerate(blocks[g])]
+                if g == p + 1:
+                    to = at + b * 8
+                    turn[to:to + 8, :] = v[b]
+                    turn[to + 8:to + 16, :] = v[b + 1]
+                    for j in range(8):
+                        s0 = turn[pl.ds(to + j, 8, stride=0), :]
+                        s1 = turn[pl.ds(to + 8 + j, 8, stride=0), :]
+                        ahead[j] = ahead[j] - (n0 * s0 + n1 * s1) * inv
                 if b < 6:
                     n0, n1 = n0 * inv, n1 * inv
                 for i in range(b + 2, 8):
@@ -307,8 +318,8 @@
                 m[g * 8:g * 8 + 8, :] = blocks[g][k]
         for j in range(8):
             emit(k0 + base + j, base + j, [t[0:1, :] for t in final[j]])
-        if p + 3 < n:
-            first = (p + 3) * 8
+        if p + 4 < n:
+            first = (p + 4) * 8
             panel = [
                 jnp.concatenate([final[j][k][0:1, :] for j in range(8)], axis=0) for k in range(len(mats))
             ]
@@ -320,7 +331,7 @@
                 m[first:, :] = m[first:, :] - less[first:, :]
 
 
-def factor_kernel(scale, g_ref, sk_ref, f_out, sk_out, a0, a1, spread, sem):
+def factor_kernel(scale, g_ref, sk_ref, f_out, sk_out, a0, a1, spread, turn, sem):
     cp = pltpu.make_async_copy(sk_ref, sk_out, sem)
     cp.start()
     lane = lax.broadcasted_iota(jnp.int32, (8, HALF), 1)
@@ -349,7 +360,7 @@
         a0[at:at + 8, :] = g_ref[at:at + 8, :] * (down[0][p] * scaled[0])
         a1[at:at + 8, :] = g_ref[128 + at:128 + at + 8, :] * (down[0][p] * scaled[1])
     f_out[128:256, 0:128] = jnp.zeros((128, 128), F32)
-    factor_block([a0, a1], spread, 0, emit(0))
+    factor_block([a0, a1], spread, turn, 0, emit(0))
     corner = f_out[0:128, 128:256]
     less = lax.dot_general(
         corner, corner, (((0,), (0,)), ((), ())), precision=lax.Precision.HIGHEST, preferred_element_type=F32
@@ -358,7 +369,7 @@
         at = p * 8
         left = g_ref[256 + at:256 + at + 8, :] - less[at:at + 8, :] * (1.0 / scale)
         a0[at:at + 8, :] = left * (down[1][p] * scaled[1])
-    factor_block([a0], spread, 128, emit(1))
+    factor_block([a0], spread, turn, 128, emit(1))
     cp.wait()
 
 
@@ -416,6 +427,7 @@
             pltpu.VMEM((HALF, HALF), F32),
             pltpu.VMEM((HALF, HALF), F32),
             pltpu.VMEM((HALF, HALF), F32),
+            pltpu.VMEM((HALF, HALF), F32),
             pltpu.SemaphoreType.DMA,
         ],
         compiler_params=pltpu.CompilerParams(vmem_limit_bytes=60 * 1024 * 1024),

time: 68.5 us -> 68.5 us (level)
  no operation moved by 1% of the time
where the time goes in v7:
time: 68.5 us; the launch traced here: 68.3 us
  Pallas kernels  67.7 us (99%)
    pallas_call x1, Pallas kernels, body(): pl.pallas_call(gram_kernel, out_shape=(jax.ShapeDtypeStruct((BPO, width),...  57 us
    pallas_call x1, Pallas kernels, body(): pl.pallas_call(lambda *refs: factor_kernel(1.0 / slots, *refs), out_shape...  10.7 us

profile of v7, /device:TPU:1, one launch (start us, length us, event | category | flops | bytes accessed | tf_op | source)
XLA Modules:
  0.0 68.3 jit_solution(1875592883651223606)
XLA Ops:
  0.6 57.0 %shard_map.59 = (f32[256,256]{1,0:T(8,128)}, f32[384,128]{1,0:T(8,128)}) custom-call(f32[4,2,4,2,8,256]{5,4,3,2,1,0:T(8,128)} %bitcast.2, s32[1,512]{1,0:T(1,128)} %buckets_hbm.1, s32[1,512]{1,0:T(1,128)} %signs_hbm.1, s32[1,128]{1,0:T(1,128)} %counts_hbm.1), custom_call_target="tpu_custom_call" | custom-call | tf_op jit(solution)/shard_map/pallas_call | solution.py:383
  57.7 10.7 %shard_map.60 = (f32[256,256]{1,0:T(8,128)}, f32[256,256]{1,0:T(8,128)}) custom-call(f32[384,128]{1,0:T(8,128)} %get-tuple-element.6.refs_0_, f32[256,256]{1,0:T(8,128)} %get-tuple-element.7.refs_1_), custom_call_target="tpu_custom_call" | custom-call | tf_op jit(solution)/shard_map/pallas_call | solution.py:421

commit v8 on v4

--- a/solution.py
+++ b/solution.py
@@ -18,7 +18,7 @@
 
 def gram_kernel(
     slab_hbm, buckets_hbm, signs_hbm, counts_hbm, sk_out, g_out,
-    slab, buckets, signs, counts, sk, meta, r1a, r1b, r2a, r2b, m1, m2, mt, gp, gx, acc, gz, part, gy, fin, gfull,
+    slab, buckets, signs, counts, sk, meta, r1a, r1b, r2a, r2b, m1, m2, mt, gp, gc, gh, gx, acc, gz, part, gy, fin, gfull,
     loc_sem, s1a_s, s1a_r, s1b_s, s1b_r, s1m_s, s1m_r, s2a_s, s2a_r, s2b_s, s2b_r, s2m_s, s2m_r,
     x_s, x_r, z_s, z_r, y_s, y_r, zg_s, zg_r, xg_s, xg_r,
 ):
@@ -198,16 +198,19 @@
     gp[pl.ds(256, 128), :] = gram[HALF:, HALF:]
 
     e = x * 2 + c
-    near = [(d, dc) for d in (2, 1, 3, 0) for dc in range(2) if d or dc]
+    sibling = dev(z, y, 1 - c, x)
+    quarters = gp.reshape(4, 96, 128)
+    rcopy(quarters.at[:, pl.ds((1 - c) * 48, 48)], gc, x_s.at[0], x_r.at[0], sibling).wait_recv()
+    for i in range(4):
+        gh[i] = gp[pl.ds(pl.multiple_of(i * 96 + c * 48, 8), 48), :] + gc[i]
     got = []
-    for d, dc in near:
-        xt, ct = (x + d) % NX, (c + dc) % 2
-        at = pl.ds((xt * 2 + ct) * 48, 48)
-        got.append(rcopy(gp.at[at], gx.at[d * 2 + dc], x_s.at[d * 2 + dc], x_r.at[d * 2 + dc], dev(z, y, ct, xt)))
-    total = gp[pl.ds(pl.multiple_of(e * 48, 8), 48), :]
-    for (d, dc), cp in reversed(list(zip(near, got))):
-        cp.wait_recv()
-        total = total + gx[d * 2 + dc]
+    for d in (2, 1, 3):
+        xt = (x + d) % NX
+        got.append(rcopy(gh.at[xt], gx.at[d], x_s.at[d], x_r.at[d], dev(z, y, c, xt)))
+    total = gh[x]
+    for d, cp in reversed(list(zip((2, 1, 3), got))):
+        cp.wait_recv()
+        total = total + gx[d]
     acc[...] = total
 
     got = []
@@ -238,14 +241,20 @@
     for cp in got:
         cp.wait_recv()
 
+    def place_of(xx):
+        return gfull.at[pl.ds((xx * 2 + c) * 48, 48)]
+
     got = []
-    for d, dc in near:
-        xt, ct = (x + d) % NX, (c + dc) % 2
-        got.append(
-            rcopy(fin, gfull.at[pl.ds(e * 48, 48)], xg_s.at[d * 2 + dc], xg_r.at[d * 2 + dc], dev(z, y, ct, xt))
-        )
+    for d in (2, 1, 3):
+        xt = (x + d) % NX
+        got.append(rcopy(fin, place_of(x), xg_s.at[d], xg_r.at[d], dev(z, y, c, xt)))
+    over = [rcopy(fin, place_of(x), xg_s.at[4], xg_r.at[4], sibling)]
     gfull[pl.ds(pl.multiple_of(e * 48, 8), 48), :] = fin[...]
-    for cp in got:
+    for d, cp in reversed(list(zip((2, 1, 3), got))):
+        cp.wait_recv()
+        piece = place_of((x + NX - d) % NX)
+        over.append(rcopy(piece, piece, xg_s.at[4 + d], xg_r.at[4 + d], sibling))
+    for cp in over:
         cp.wait_recv()
     g_out[...] = gfull[...]
     save.wait()
@@ -389,6 +398,8 @@
             pltpu.VMEM((2, 8, 8, 128), jnp.int32),
             pltpu.VMEM((128, 128), jnp.int32),
             pltpu.VMEM((384, 128), F32),
+            pltpu.VMEM((4, 48, 128), F32),
+            pltpu.VMEM((4, 48, 128), F32),
             pltpu.VMEM((8, 48, 128), F32),
             pltpu.VMEM((48, 128), F32),
             pltpu.VMEM((8, 8, 128), F32),

time: 68.5 us -> 69.8 us (1.019)
  Pallas kernels: 67.7 us -> 69 us
    pallas_call x1, Pallas kernels: 57 us -> 58.3 us  [body(): pl.pallas_call(gram_kernel, out_shape=(jax.ShapeDtypeStruct((BPO, width),...]
where the time goes in v8:
time: 69.8 us; the launch traced here: 69.7 us
  Pallas kernels  69 us (99%)
    pallas_call x1, Pallas kernels, body(): pl.pallas_call(gram_kernel, out_shape=(jax.ShapeDtypeStruct((BPO, width),...  58.3 us
    pallas_call x1, Pallas kernels, body(): pl.pallas_call(lambda *refs: factor_kernel(1.0 / slots, *refs), out_shape...  10.7 us

profile of v8, /device:TPU:1, one launch (start us, length us, event | category | flops | bytes accessed | tf_op | source)
XLA Modules:
  0.0 69.7 jit_solution(14306564363381093418)
XLA Ops:
  0.6 58.3 %shard_map.59 = (f32[256,256]{1,0:T(8,128)}, f32[384,128]{1,0:T(8,128)}) custom-call(f32[4,2,4,2,8,256]{5,4,3,2,1,0:T(8,128)} %bitcast.2, s32[1,512]{1,0:T(1,128)} %buckets_hbm.1, s32[1,512]{1,0:T(1,128)} %signs_hbm.1, s32[1,128]{1,0:T(1,128)} %counts_hbm.1), custom_call_target="tpu_custom_call" | custom-call | tf_op jit(solution)/shard_map/pallas_call | solution.py:381
  59.0 10.7 %shard_map.60 = (f32[256,256]{1,0:T(8,128)}, f32[256,256]{1,0:T(8,128)}) custom-call(f32[384,128]{1,0:T(8,128)} %get-tuple-element.6.refs_0_, f32[256,256]{1,0:T(8,128)} %get-tuple-element.7.refs_1_), custom_call_target="tpu_custom_call" | custom-call | tf_op jit(solution)/shard_map/pallas_call | solution.py:421

commit v9 on v4

--- a/solution.py
+++ b/solution.py
@@ -40,6 +40,17 @@
     for d in range(1, 4):
         for dc in range(2):
             peers.append(dev(z, y, (c + dc) % 2, (x + d) % NX))
+    def lcopy(src, dst, sem):
+        cp = pltpu.make_async_copy(src, dst, sem)
+        cp.start()
+        return cp
+
+    load = lcopy(slab_hbm, slab, loc_sem.at[2])
+    small = [
+        lcopy(counts_hbm, counts, loc_sem.at[5]),
+        lcopy(signs_hbm, signs, loc_sem.at[6]),
+        lcopy(buckets_hbm, buckets, loc_sem.at[7]),
+    ]
     for p in peers:
         pl.semaphore_signal(barrier, inc=1, device_id=p, device_id_type=MESH)
 
@@ -53,17 +64,6 @@
         sends.append(cp)
         return cp
 
-    def lcopy(src, dst, sem):
-        cp = pltpu.make_async_copy(src, dst, sem)
-        cp.start()
-        return cp
-
-    load = lcopy(slab_hbm, slab, loc_sem.at[2])
-    small = [
-        lcopy(counts_hbm, counts, loc_sem.at[5]),
-        lcopy(signs_hbm, signs, loc_sem.at[6]),
-        lcopy(buckets_hbm, buckets, loc_sem.at[7]),
-    ]
     slot = lax.broadcasted_iota(jnp.int32, (HALF, 512), 1)
     pair = lax.broadcasted_iota(jnp.int32, (HALF, 512), 0)
     spread = jnp.where(slot // 4 == pair, 1.0, 0.0).astype(BF16)

time: 68.5 us -> 68.5 us (level)
  no operation moved by 1% of the time
where the time goes in v9:
time: 68.5 us; the launch traced here: 68.3 us
  Pallas kernels  67.7 us (99%)
    pallas_call x1, Pallas kernels, body(): pl.pallas_call(gram_kernel, out_shape=(jax.ShapeDtypeStruct((BPO, width),...  57 us
    pallas_call x1, Pallas kernels, body(): pl.pallas_call(lambda *refs: factor_kernel(1.0 / slots, *refs), out_shape...  10.7 us

profile of v9, /device:TPU:1, one launch (start us, length us, event | category | flops | bytes accessed | tf_op | source)
XLA Modules:
  0.0 68.3 jit_solution(342281436538401357)
XLA Ops:
  0.6 57.0 %shard_map.59 = (f32[256,256]{1,0:T(8,128)}, f32[384,128]{1,0:T(8,128)}) custom-call(f32[4,2,4,2,8,256]{5,4,3,2,1,0:T(8,128)} %bitcast.2, s32[1,512]{1,0:T(1,128)} %buckets_hbm.1, s32[1,512]{1,0:T(1,128)} %signs_hbm.1, s32[1,128]{1,0:T(1,128)} %counts_hbm.1), custom_call_target="tpu_custom_call" | custom-call | tf_op jit(solution)/shard_map/pallas_call | solution.py:372
  57.7 10.7 %shard_map.60 = (f32[256,256]{1,0:T(8,128)}, f32[256,256]{1,0:T(8,128)}) custom-call(f32[384,128]{1,0:T(8,128)} %get-tuple-element.6.refs_0_, f32[256,256]{1,0:T(8,128)} %get-tuple-element.7.refs_1_), custom_call_target="tpu_custom_call" | custom-call | tf_op jit(solution)/shard_map/pallas_call | solution.py:410
